TPU v7x, 32 devices: a whole 2x2x4 slice. The times are simulated.
32 devices in a mesh: dp: 4 (over y, x), seq: 8 (over z, core).
Axes of the slice: x: 2, y: 2, z: 4, core: 2. Of those that a mesh axis runs over, the one named last changes fastest.
Arguments:
- queries: bfloat16 [4096, 32, 128], P(('dp', 'seq')), parts along dimension 0, may hold values from -6 to 6
- keys: bfloat16 [4096, 4, 128], P(('dp', 'seq')), parts along dimension 0, may hold values from -6 to 6
- values: bfloat16 [4096, 4, 128], P(('dp', 'seq')), parts along dimension 0, may hold values from -6 to 6
- attn_out: bfloat16 [4096, 32, 128], P(('dp', 'seq')), parts along dimension 0, may hold values from -6 to 6
- out_grad: bfloat16 [4096, 32, 128], P(('dp', 'seq')), parts along dimension 0, may hold values from -1.5 to 1.5
- log_sums: float32 [32, 4096], P(None, ('dp', 'seq')), parts along dimension 1, may hold values from 2 to 4
- doc_ids: int32 [4096], P('dp'), parts along dimension 0, may hold values from 0 to 3, never falling along the last dimension, each value on 1 to 512 neighbouring positions
Outputs:
- query_grad: bfloat16 [4096, 32, 128], P(('dp', 'seq')), parts along dimension 0
- key_grad: bfloat16 [4096, 4, 128], P(('dp', 'seq')), parts along dimension 0
- value_grad: bfloat16 [4096, 4, 128], P(('dp', 'seq')), parts along dimension 0
There are 4 independent parts, one for each index of `dp`. A program takes and returns all parts, laid end to end along the dimension named above; each array names one. Nothing has to cross between parts.
Inputs may be any that keep to these rules, and one draw needn't show every extreme that they name: `doc_ids`: document numbers never fall along the sequence; each document holds 1 to 512 positions, and one holds exactly 512.
All inputs are finite; a program needn't handle non-finite values.
Results may differ from a plain program's by a relative error of at most 0.009.
Values may be sent and summed in bfloat16 or wider, within the bound.
No kernel may reach another device: no remote copies, remote signals or barrier semaphores. Data moves between devices by JAX's collectives and lax.ppermute only.
A program may use at most 64 MiB of HBM per device.

v0:
```python
import jax
import jax.numpy as jnp
from jax import lax
from jax.sharding import PartitionSpec as P

REACH = 4


def from_behind(value, axis, steps):
    count = lax.axis_size(axis)
    initial, last = (max(0, -steps), min(count, count - steps))
    return lax.ppermute(value, axis, [(source, source + steps) for source in range(initial, last)])


def on_device(queries, keys, values, attn_out, out_grad, log_sums, doc_ids):
    width = queries.shape[0]
    heads = queries.shape[1]
    head_size = queries.shape[2]
    kv_count = keys.shape[1]
    group = heads // kv_count
    scale = head_size ** (-0.5)
    shard = lax.axis_index("seq")
    delta = jnp.sum(out_grad.astype(jnp.float32) * attn_out.astype(jnp.float32), axis=-1).T.reshape(
        kv_count, group, width
    )
    log_blk = log_sums.reshape(kv_count, group, width)
    query_grp = queries.reshape(width, kv_count, group, head_size)
    grad_grp = out_grad.reshape(width, kv_count, group, head_size)
    offsets = jnp.arange(width, dtype=jnp.int32)
    query_pos = shard * width + offsets
    query_doc = lax.dynamic_slice_in_dim(doc_ids, shard * width, width, 0)

    def live_mask(distance):
        key_start = (shard - distance) * width
        key_pos = key_start + offsets
        key_doc = lax.dynamic_slice_in_dim(doc_ids, jnp.maximum(key_start, 0), width, 0)
        return (
            (key_pos[None, :] <= query_pos[:, None])
            & (key_doc[None, :] == query_doc[:, None])
            & (key_pos[None, :] >= 0)
        )

    def gradients(key_blk, val_blk, live):
        scores = (
            jnp.einsum("tkgd,skd->kgts", query_grp, key_blk, preferred_element_type=jnp.float32)
            * scale
        )
        probs = jnp.where(live, jnp.exp(scores - log_blk[..., None]), 0.0)
        dprobs = jnp.einsum("tkgd,skd->kgts", grad_grp, val_blk, preferred_element_type=jnp.float32)
        dscores = (probs * (dprobs - delta[..., None])).astype(jnp.bfloat16)
        probs_low = probs.astype(jnp.bfloat16)
        query_part = (
            jnp.einsum("kgts,skd->tkgd", dscores, key_blk, preferred_element_type=jnp.float32)
            * scale
        )
        key_part = (
            jnp.einsum("kgts,tkgd->skd", dscores, query_grp, preferred_element_type=jnp.float32)
            * scale
        )
        val_part = jnp.einsum(
            "kgts,tkgd->skd", probs_low, grad_grp, preferred_element_type=jnp.float32
        )
        return (query_part, key_part.astype(jnp.bfloat16), val_part.astype(jnp.bfloat16))

    key_list = []
    val_list = []
    for distance in range(1, REACH + 1):
        key_got, val_got = from_behind((keys, values), "seq", distance)
        key_list.append(key_got)
        val_list.append(val_got)
    key_far = jnp.stack(key_list)
    val_far = jnp.stack(val_list)
    query_total, key_own, val_own = gradients(keys, values, live_mask(0))
    key_parts = []
    val_parts = []
    for distance in range(1, REACH + 1):
        live = live_mask(distance)
        key_blk = key_far[distance - 1]
        val_blk = val_far[distance - 1]
        query_part, key_part, val_part = gradients(key_blk, val_blk, live)
        query_total = query_total + query_part
        key_parts.append(key_part)
        val_parts.append(val_part)
    key_stack = jnp.stack(key_parts)
    val_stack = jnp.stack(val_parts)
    key_total = key_own.astype(jnp.float32)
    val_total = val_own.astype(jnp.float32)
    for distance in range(1, REACH + 1):
        key_back, val_back = from_behind(
            (key_stack[distance - 1], val_stack[distance - 1]), "seq", -distance
        )
        key_total = key_total + key_back.astype(jnp.float32)
        val_total = val_total + val_back.astype(jnp.float32)
    query_grad = query_total.reshape(width, heads, head_size).astype(jnp.bfloat16)
    return (query_grad, key_total.astype(jnp.bfloat16), val_total.astype(jnp.bfloat16))


def solution(mesh):
    placed = (
        P(("dp", "seq"), None, None),
        P(("dp", "seq"), None, None),
        P(("dp", "seq"), None, None),
        P(("dp", "seq"), None, None),
        P(("dp", "seq"), None, None),
        P(None, ("dp", "seq")),
        P("dp"),
    )
    return jax.shard_map(
        on_device,
        mesh=mesh,
        in_specs=placed,
        out_specs=(
            P(("dp", "seq"), None, None),
            P(("dp", "seq"), None, None),
            P(("dp", "seq"), None, None),
        ),
        check_vma=False,
    )
```

profile of v0, /device:TPU:0, one launch (start us, length us, event | category | flops | bytes accessed | tf_op | source)
XLA Modules:
  0.0 81.6 jit_solution(5822397177884110991)
XLA Ops:
  0.6 0.0 copy-start
  0.6 0.0 copy-start.3
  0.7 1.0 %copy.98 = bf16[128,4,128]{2,0,1:T(8,128)(2,1)S(1)} copy(bf16[128,4,128]{2,1,0:T(4,128)(2,1)} %param.9) | data formatting | bytes 262144 | tf_op args[2]
  1.7 5.9 %collective-permute-start.7 = (bf16[128,4,128]{2,0,1:T(8,128)(2,1)S(1)}, bf16[128,4,128]{2,0,1:T(8,128)(2,1)S(1)}, u32[]{:S(2)}, u32[]{:S(2)}) collective-permute-start(bf16[128,4,128]{2,0,1:T(8,128)(2,1)S(1)} %copy.98), channel_id=1, source_target_pairs={{0,4},{1,5},{2,6},{3,7},{8,12},{9,13},{10,14},{11,15},{16,20},{17,... | collective-permute-start | bytes 393224 | tf_op jit(solution)/shard_map/ppermute | solution.py:12
  7.7 2.6 %collective-permute-start.5 = (bf16[128,4,128]{2,0,1:T(8,128)(2,1)S(1)}, bf16[128,4,128]{2,0,1:T(8,128)(2,1)S(1)}, u32[]{:S(2)}, u32[]{:S(2)}) collective-permute-start(bf16[128,4,128]{2,0,1:T(8,128)(2,1)S(1)} %copy.98), channel_id=1, source_target_pairs={{0,3},{1,4},{2,5},{3,6},{4,7},{8,11},{9,12},{10,13},{11,14},{12,15... | collective-permute-start | bytes 393224 | tf_op jit(solution)/shard_map/ppermute | solution.py:12
  10.3 2.1 %collective-permute-start.3 = (bf16[128,4,128]{2,0,1:T(8,128)(2,1)S(1)}, bf16[128,4,128]{2,0,1:T(8,128)(2,1)S(1)}, u32[]{:S(2)}, u32[]{:S(2)}) collective-permute-start(bf16[128,4,128]{2,0,1:T(8,128)(2,1)S(1)} %copy.98), channel_id=1, source_target_pairs={{0,2},{1,3},{2,4},{3,5},{4,6},{5,7},{8,10},{9,11},{10,12},{11,13},... | collective-permute-start | bytes 393224 | tf_op jit(solution)/shard_map/ppermute | solution.py:12
  12.5 1.8 %collective-permute-start.1 = (bf16[128,4,128]{2,0,1:T(8,128)(2,1)S(1)}, bf16[128,4,128]{2,0,1:T(8,128)(2,1)S(1)}, u32[]{:S(2)}, u32[]{:S(2)}) collective-permute-start(bf16[128,4,128]{2,0,1:T(8,128)(2,1)S(1)} %copy.98), channel_id=1, source_target_pairs={{0,1},{1,2},{2,3},{3,4},{4,5},{5,6},{6,7},{8,9},{9,10},{10,11},{11... | collective-permute-start | bytes 393224 | tf_op jit(solution)/shard_map/ppermute | solution.py:12
  14.3 0.9 %copy.96 = bf16[128,4,128]{2,0,1:T(8,128)(2,1)S(1)} copy(bf16[128,4,128]{2,1,0:T(4,128)(2,1)} %param.8) | data formatting | bytes 262144 | tf_op args[1]
  15.2 2.1 %collective-permute-start = (bf16[128,4,128]{2,0,1:T(8,128)(2,1)S(1)}, bf16[128,4,128]{2,0,1:T(8,128)(2,1)S(1)}, u32[]{:S(2)}, u32[]{:S(2)}) collective-permute-start(bf16[128,4,128]{2,0,1:T(8,128)(2,1)S(1)} %copy.96), channel_id=1, source_target_pairs={{0,1},{1,2},{2,3},{3,4},{4,5},{5,6},{6,7},{8,9},{9,10},{10,11},{11... | collective-permute-start | bytes 393224 | tf_op jit(solution)/shard_map/ppermute | solution.py:12
  17.4 2.2 %multiply_reduce_fusion = f32[128,32]{1,0:T(8,128)S(1)} fusion(bf16[128,32,128]{2,1,0:T(8,128)(2,1)} %param.10, bf16[128,32,128]{2,1,0:T(8,128)(2,1)} %param.11), kind=kLoop, calls=%fused_computation.31 | loop fusion | flops 2093056 | bytes 2113536 | tf_op jit(solution)/shard_map/reduce_sum | solution.py:23
  19.6 0.0 copy-start.1
  19.6 0.0 copy-start.2
  19.6 0.1 copy.93
  19.7 0.1 fusion.98
  19.8 0.3 and_and_fusion
  20.1 0.8 fusion.19
  21.0 0.6 fusion.17
  21.6 0.5 fusion.71
  22.1 2.0 %collective-permute-start.2 = (bf16[128,4,128]{2,0,1:T(8,128)(2,1)S(1)}, bf16[128,4,128]{2,0,1:T(8,128)(2,1)S(1)}, u32[]{:S(2)}, u32[]{:S(2)}) collective-permute-start(bf16[128,4,128]{2,0,1:T(8,128)(2,1)S(1)} %copy.96), channel_id=1, source_target_pairs={{0,2},{1,3},{2,4},{3,5},{4,6},{5,7},{8,10},{9,11},{10,12},{11,13},... | collective-permute-start | bytes 393224 | tf_op jit(solution)/shard_map/ppermute | solution.py:12
  24.1 0.8 fusion.15
  24.9 0.6 fusion.46
  25.5 1.1 %collective-permute-done.2 = bf16[128,4,128]{2,0,1:T(8,128)(2,1)S(1)} collective-permute-done((bf16[128,4,128]{2,0,1:T(8,128)(2,1)S(1)}, bf16[128,4,128]{2,0,1:T(8,128)(2,1)S(1)}, u32[]{:S(2)}, u32[]{:S(2)}) %collective-permute-start.2) | collective-permute-done | bytes 131104 | tf_op jit(solution)/shard_map/ppermute | solution.py:12
  26.6 8.6 %collective-permute-start.6 = (bf16[128,4,128]{2,0,1:T(8,128)(2,1)S(1)}, bf16[128,4,128]{2,0,1:T(8,128)(2,1)S(1)}, u32[]{:S(2)}, u32[]{:S(2)}) collective-permute-start(bf16[128,4,128]{2,0,1:T(8,128)(2,1)S(1)} %copy.96), channel_id=1, source_target_pairs={{0,4},{1,5},{2,6},{3,7},{8,12},{9,13},{10,14},{11,15},{16,20},{17,... | collective-permute-start | bytes 393224 | tf_op jit(solution)/shard_map/ppermute | solution.py:12
  35.2 0.8 fusion.11
  36.0 0.6 fusion.45
  36.6 0.0 collective-permute-done.1
  36.6 1.3 %collective-permute-start.4 = (bf16[128,4,128]{2,0,1:T(8,128)(2,1)S(1)}, bf16[128,4,128]{2,0,1:T(8,128)(2,1)S(1)}, u32[]{:S(2)}, u32[]{:S(2)}) collective-permute-start(bf16[128,4,128]{2,0,1:T(8,128)(2,1)S(1)} %copy.96), channel_id=1, source_target_pairs={{0,3},{1,4},{2,5},{3,6},{4,7},{8,11},{9,12},{10,13},{11,14},{12,15... | collective-permute-start | bytes 393224 | tf_op jit(solution)/shard_map/ppermute | solution.py:12
  37.9 0.7 fusion.13
  38.6 0.6 fusion.42
  39.2 2.0 %collective-permute-done.4 = bf16[128,4,128]{2,0,1:T(8,128)(2,1)S(1)} collective-permute-done((bf16[128,4,128]{2,0,1:T(8,128)(2,1)S(1)}, bf16[128,4,128]{2,0,1:T(8,128)(2,1)S(1)}, u32[]{:S(2)}, u32[]{:S(2)}) %collective-permute-start.4) | collective-permute-done | bytes 131104 | tf_op jit(solution)/shard_map/ppermute | solution.py:12
  41.2 1.3 %collective-permute-start.8 = (bf16[128,4,128]{2,0,1:T(8,128)(2,1)S(1)}, bf16[128,4,128]{2,0,1:T(8,128)(2,1)S(1)}, u32[]{:S(2)}, u32[]{:S(2)}) collective-permute-start(bf16[128,4,128]{2,0,1:T(8,128)(2,1)S(1)} %fusion.42), channel_id=1, source_target_pairs={{1,0},{2,1},{3,2},{4,3},{5,4},{6,5},{7,6},{9,8},{10,9},{11,10},{12... | collective-permute-start | bytes 393224 | tf_op jit(solution)/shard_map/ppermute | solution.py:12
  42.5 0.8 fusion.7
  43.3 0.6 fusion.44
  43.9 1.3 %collective-permute-start.12 = (bf16[128,4,128]{2,0,1:T(8,128)(2,1)S(1)}, bf16[128,4,128]{2,0,1:T(8,128)(2,1)S(1)}, u32[]{:S(2)}, u32[]{:S(2)}) collective-permute-start(bf16[128,4,128]{2,0,1:T(8,128)(2,1)S(1)} %fusion.46), channel_id=1, source_target_pairs={{1,0},{2,1},{3,2},{4,3},{5,4},{6,5},{7,6},{9,8},{10,9},{11,10},{12... | collective-permute-start | bytes 393224 | tf_op jit(solution)/shard_map/ppermute | solution.py:12
  45.2 0.7 fusion.9
  45.9 0.6 fusion.41
  46.4 0.0 collective-permute-done.5
  46.5 1.3 %collective-permute-start.9 = (bf16[128,4,128]{2,0,1:T(8,128)(2,1)S(1)}, bf16[128,4,128]{2,0,1:T(8,128)(2,1)S(1)}, u32[]{:S(2)}, u32[]{:S(2)}) collective-permute-start(bf16[128,4,128]{2,0,1:T(8,128)(2,1)S(1)} %fusion.41), channel_id=1, source_target_pairs={{2,0},{3,1},{4,2},{5,3},{6,4},{7,5},{10,8},{11,9},{12,10},{13,11},... | collective-permute-start | bytes 393224 | tf_op jit(solution)/shard_map/ppermute | solution.py:12
  47.8 0.7 fusion.5
  48.4 0.6 fusion.40
  49.0 1.5 %collective-permute-start.10 = (bf16[128,4,128]{2,0,1:T(8,128)(2,1)S(1)}, bf16[128,4,128]{2,0,1:T(8,128)(2,1)S(1)}, u32[]{:S(2)}, u32[]{:S(2)}) collective-permute-start(bf16[128,4,128]{2,0,1:T(8,128)(2,1)S(1)} %fusion.40), channel_id=1, source_target_pairs={{3,0},{4,1},{5,2},{6,3},{7,4},{11,8},{12,9},{13,10},{14,11},{15,12... | collective-permute-start | bytes 393224 | tf_op jit(solution)/shard_map/ppermute | solution.py:12
  50.5 0.8 fusion.3
  51.3 0.6 fusion.43
  51.9 0.0 collective-permute-done.7
  51.9 0.7 fusion.1
  52.6 0.6 fusion.39
  53.2 1.3 %collective-permute-start.11 = (bf16[128,4,128]{2,0,1:T(8,128)(2,1)S(1)}, bf16[128,4,128]{2,0,1:T(8,128)(2,1)S(1)}, u32[]{:S(2)}, u32[]{:S(2)}) collective-permute-start(bf16[128,4,128]{2,0,1:T(8,128)(2,1)S(1)} %fusion.39), channel_id=1, source_target_pairs={{4,0},{5,1},{6,2},{7,3},{12,8},{13,9},{14,10},{15,11},{20,16},{21,... | collective-permute-start | bytes 393224 | tf_op jit(solution)/shard_map/ppermute | solution.py:12
  54.5 0.5 fusion.67
  55.0 0.5 fusion.63
  55.6 0.5 fusion.59
  56.1 0.7 multiply_convert_fusion
  56.8 1.6 %copy.126 = bf16[128,32,128]{2,1,0:T(8,128)(2,1)} copy(bf16[128,32,128]{2,0,1:T(8,128)(2,1)S(1)} %bitcast.263) | data formatting | bytes 2097152
  58.5 0.0 collective-permute-done.8
  58.5 1.3 %collective-permute-start.13 = (bf16[128,4,128]{2,0,1:T(8,128)(2,1)S(1)}, bf16[128,4,128]{2,0,1:T(8,128)(2,1)S(1)}, u32[]{:S(2)}, u32[]{:S(2)}) collective-permute-start(bf16[128,4,128]{2,0,1:T(8,128)(2,1)S(1)} %fusion.45), channel_id=1, source_target_pairs={{2,0},{3,1},{4,2},{5,3},{6,4},{7,5},{10,8},{11,9},{12,10},{13,11},... | collective-permute-start | bytes 393224 | tf_op jit(solution)/shard_map/ppermute | solution.py:12
  59.8 1.3 %collective-permute-start.14 = (bf16[128,4,128]{2,0,1:T(8,128)(2,1)S(1)}, bf16[128,4,128]{2,0,1:T(8,128)(2,1)S(1)}, u32[]{:S(2)}, u32[]{:S(2)}) collective-permute-start(bf16[128,4,128]{2,0,1:T(8,128)(2,1)S(1)} %fusion.44), channel_id=1, source_target_pairs={{3,0},{4,1},{5,2},{6,3},{7,4},{11,8},{12,9},{13,10},{14,11},{15,12... | collective-permute-start | bytes 393224 | tf_op jit(solution)/shard_map/ppermute | solution.py:12
  61.1 1.3 %collective-permute-start.15 = (bf16[128,4,128]{2,0,1:T(8,128)(2,1)S(1)}, bf16[128,4,128]{2,0,1:T(8,128)(2,1)S(1)}, u32[]{:S(2)}, u32[]{:S(2)}) collective-permute-start(bf16[128,4,128]{2,0,1:T(8,128)(2,1)S(1)} %fusion.43), channel_id=1, source_target_pairs={{4,0},{5,1},{6,2},{7,3},{12,8},{13,9},{14,10},{15,11},{20,16},{21,... | collective-permute-start | bytes 393224 | tf_op jit(solution)/shard_map/ppermute | solution.py:12
  62.4 5.0 %collective-permute-done.11 = bf16[128,4,128]{2,0,1:T(8,128)(2,1)S(1)} collective-permute-done((bf16[128,4,128]{2,0,1:T(8,128)(2,1)S(1)}, bf16[128,4,128]{2,0,1:T(8,128)(2,1)S(1)}, u32[]{:S(2)}, u32[]{:S(2)}) %collective-permute-start.11) | collective-permute-done | bytes 131104 | tf_op jit(solution)/shard_map/ppermute | solution.py:12
  67.4 0.6 add_convert_fusion.1
  68.0 0.8 copy.127
  68.8 1.1 %collective-permute-done.13 = bf16[128,4,128]{2,0,1:T(8,128)(2,1)S(1)} collective-permute-done((bf16[128,4,128]{2,0,1:T(8,128)(2,1)S(1)}, bf16[128,4,128]{2,0,1:T(8,128)(2,1)S(1)}, u32[]{:S(2)}, u32[]{:S(2)}) %collective-permute-start.13) | collective-permute-done | bytes 131104 | tf_op jit(solution)/shard_map/ppermute | solution.py:12
  69.9 2.1 %collective-permute-done.14 = bf16[128,4,128]{2,0,1:T(8,128)(2,1)S(1)} collective-permute-done((bf16[128,4,128]{2,0,1:T(8,128)(2,1)S(1)}, bf16[128,4,128]{2,0,1:T(8,128)(2,1)S(1)}, u32[]{:S(2)}, u32[]{:S(2)}) %collective-permute-start.14) | collective-permute-done | bytes 131104 | tf_op jit(solution)/shard_map/ppermute | solution.py:12
  71.9 8.3 %collective-permute-done.15 = bf16[128,4,128]{2,0,1:T(8,128)(2,1)S(1)} collective-permute-done((bf16[128,4,128]{2,0,1:T(8,128)(2,1)S(1)}, bf16[128,4,128]{2,0,1:T(8,128)(2,1)S(1)}, u32[]{:S(2)}, u32[]{:S(2)}) %collective-permute-start.15) | collective-permute-done | bytes 131104 | tf_op jit(solution)/shard_map/ppermute | solution.py:12
  80.2 0.6 add_convert_fusion
  80.8 0.8 copy.128
  (19 shorter events, 0.1 us)
Async XLA Ops:
  0.6 19.5 %copy-start = (bf16[128,32,128]{2,1,0:T(8,128)(2,1)S(1)}, bf16[128,32,128]{2,1,0:T(8,128)(2,1)}, u32[]{:S(2)}) copy-start(bf16[128,32,128]{2,1,0:T(8,128)(2,1)} %param.7) | copy-start | bytes 3145732
  0.6 19.5 %copy-start.3 = (bf16[128,4,128]{2,1,0:T(4,128)(2,1)S(1)}, bf16[128,4,128]{2,1,0:T(4,128)(2,1)}, u32[]{:S(2)}) copy-start(bf16[128,4,128]{2,1,0:T(4,128)(2,1)} %param.8) | copy-start | bytes 393220
  0.7 19.0 %copy-start.4 = (s32[1024]{0:T(1024)S(1)}, s32[1024]{0:T(1024)}, u32[]{:S(2)}) copy-start(s32[1024]{0:T(1024)} %param.13) | copy-start | bytes 12292
  0.7 19.5 %copy-start.5 = (f32[32,128]{1,0:T(8,128)S(1)}, f32[32,128]{1,0:T(8,128)}, u32[]{:S(2)}) copy-start(f32[32,128]{1,0:T(8,128)} %param.12) | copy-start | bytes 49156
  1.7 50.2 %collective-permute-start.7 = (bf16[128,4,128]{2,0,1:T(8,128)(2,1)S(1)}, bf16[128,4,128]{2,0,1:T(8,128)(2,1)S(1)}, u32[]{:S(2)}, u32[]{:S(2)}) collective-permute-start(bf16[128,4,128]{2,0,1:T(8,128)(2,1)S(1)} %copy.98), channel_id=1, source_target_pairs={{0,4},{1,5},{2,6},{3,7},{8,12},{9,13},{10,14},{11,15},{16,20},{17,... | collective-permute-start | bytes 393224 | tf_op jit(solution)/shard_map/ppermute | solution.py:12
  7.7 38.8 %collective-permute-start.5 = (bf16[128,4,128]{2,0,1:T(8,128)(2,1)S(1)}, bf16[128,4,128]{2,0,1:T(8,128)(2,1)S(1)}, u32[]{:S(2)}, u32[]{:S(2)}) collective-permute-start(bf16[128,4,128]{2,0,1:T(8,128)(2,1)S(1)} %copy.98), channel_id=1, source_target_pairs={{0,3},{1,4},{2,5},{3,6},{4,7},{8,11},{9,12},{10,13},{11,14},{12,15... | collective-permute-start | bytes 393224 | tf_op jit(solution)/shard_map/ppermute | solution.py:12
  10.3 33.6 %collective-permute-start.3 = (bf16[128,4,128]{2,0,1:T(8,128)(2,1)S(1)}, bf16[128,4,128]{2,0,1:T(8,128)(2,1)S(1)}, u32[]{:S(2)}, u32[]{:S(2)}) collective-permute-start(bf16[128,4,128]{2,0,1:T(8,128)(2,1)S(1)} %copy.98), channel_id=1, source_target_pairs={{0,2},{1,3},{2,4},{3,5},{4,6},{5,7},{8,10},{9,11},{10,12},{11,13},... | collective-permute-start | bytes 393224 | tf_op jit(solution)/shard_map/ppermute | solution.py:12
  12.5 24.2 %collective-permute-start.1 = (bf16[128,4,128]{2,0,1:T(8,128)(2,1)S(1)}, bf16[128,4,128]{2,0,1:T(8,128)(2,1)S(1)}, u32[]{:S(2)}, u32[]{:S(2)}) collective-permute-start(bf16[128,4,128]{2,0,1:T(8,128)(2,1)S(1)} %copy.98), channel_id=1, source_target_pairs={{0,1},{1,2},{2,3},{3,4},{4,5},{5,6},{6,7},{8,9},{9,10},{10,11},{11... | collective-permute-start | bytes 393224 | tf_op jit(solution)/shard_map/ppermute | solution.py:12
  15.2 6.9 %collective-permute-start = (bf16[128,4,128]{2,0,1:T(8,128)(2,1)S(1)}, bf16[128,4,128]{2,0,1:T(8,128)(2,1)S(1)}, u32[]{:S(2)}, u32[]{:S(2)}) collective-permute-start(bf16[128,4,128]{2,0,1:T(8,128)(2,1)S(1)} %copy.96), channel_id=1, source_target_pairs={{0,1},{1,2},{2,3},{3,4},{4,5},{5,6},{6,7},{8,9},{9,10},{10,11},{11... | collective-permute-start | bytes 393224 | tf_op jit(solution)/shard_map/ppermute | solution.py:12
  19.6 1.3 %copy-start.1 = (bf16[128,32,128]{2,1,0:T(8,128)(2,1)S(1)}, bf16[128,32,128]{2,1,0:T(8,128)(2,1)}, u32[]{:S(2)}) copy-start(bf16[128,32,128]{2,1,0:T(8,128)(2,1)} %param.11) | copy-start | bytes 3145732
  19.6 1.3 %copy-start.2 = (bf16[128,4,128]{2,1,0:T(4,128)(2,1)S(1)}, bf16[128,4,128]{2,1,0:T(4,128)(2,1)}, u32[]{:S(2)}) copy-start(bf16[128,4,128]{2,1,0:T(4,128)(2,1)} %param.9) | copy-start | bytes 393220
  22.1 4.5 %collective-permute-start.2 = (bf16[128,4,128]{2,0,1:T(8,128)(2,1)S(1)}, bf16[128,4,128]{2,0,1:T(8,128)(2,1)S(1)}, u32[]{:S(2)}, u32[]{:S(2)}) collective-permute-start(bf16[128,4,128]{2,0,1:T(8,128)(2,1)S(1)} %copy.96), channel_id=1, source_target_pairs={{0,2},{1,3},{2,4},{3,5},{4,6},{5,7},{8,10},{9,11},{10,12},{11,13},... | collective-permute-start | bytes 393224 | tf_op jit(solution)/shard_map/ppermute | solution.py:12
  26.6 22.4 %collective-permute-start.6 = (bf16[128,4,128]{2,0,1:T(8,128)(2,1)S(1)}, bf16[128,4,128]{2,0,1:T(8,128)(2,1)S(1)}, u32[]{:S(2)}, u32[]{:S(2)}) collective-permute-start(bf16[128,4,128]{2,0,1:T(8,128)(2,1)S(1)} %copy.96), channel_id=1, source_target_pairs={{0,4},{1,5},{2,6},{3,7},{8,12},{9,13},{10,14},{11,15},{16,20},{17,... | collective-permute-start | bytes 393224 | tf_op jit(solution)/shard_map/ppermute | solution.py:12
  36.6 4.6 %collective-permute-start.4 = (bf16[128,4,128]{2,0,1:T(8,128)(2,1)S(1)}, bf16[128,4,128]{2,0,1:T(8,128)(2,1)S(1)}, u32[]{:S(2)}, u32[]{:S(2)}) collective-permute-start(bf16[128,4,128]{2,0,1:T(8,128)(2,1)S(1)} %copy.96), channel_id=1, source_target_pairs={{0,3},{1,4},{2,5},{3,6},{4,7},{8,11},{9,12},{10,13},{11,14},{12,15... | collective-permute-start | bytes 393224 | tf_op jit(solution)/shard_map/ppermute | solution.py:12
  41.2 17.3 %collective-permute-start.8 = (bf16[128,4,128]{2,0,1:T(8,128)(2,1)S(1)}, bf16[128,4,128]{2,0,1:T(8,128)(2,1)S(1)}, u32[]{:S(2)}, u32[]{:S(2)}) collective-permute-start(bf16[128,4,128]{2,0,1:T(8,128)(2,1)S(1)} %fusion.42), channel_id=1, source_target_pairs={{1,0},{2,1},{3,2},{4,3},{5,4},{6,5},{7,6},{9,8},{10,9},{11,10},{12... | collective-permute-start | bytes 393224 | tf_op jit(solution)/shard_map/ppermute | solution.py:12
  43.9 24.9 %collective-permute-start.12 = (bf16[128,4,128]{2,0,1:T(8,128)(2,1)S(1)}, bf16[128,4,128]{2,0,1:T(8,128)(2,1)S(1)}, u32[]{:S(2)}, u32[]{:S(2)}) collective-permute-start(bf16[128,4,128]{2,0,1:T(8,128)(2,1)S(1)} %fusion.46), channel_id=1, source_target_pairs={{1,0},{2,1},{3,2},{4,3},{5,4},{6,5},{7,6},{9,8},{10,9},{11,10},{12... | collective-permute-start | bytes 393224 | tf_op jit(solution)/shard_map/ppermute | solution.py:12
  46.5 13.3 %collective-permute-start.9 = (bf16[128,4,128]{2,0,1:T(8,128)(2,1)S(1)}, bf16[128,4,128]{2,0,1:T(8,128)(2,1)S(1)}, u32[]{:S(2)}, u32[]{:S(2)}) collective-permute-start(bf16[128,4,128]{2,0,1:T(8,128)(2,1)S(1)} %fusion.41), channel_id=1, source_target_pairs={{2,0},{3,1},{4,2},{5,3},{6,4},{7,5},{10,8},{11,9},{12,10},{13,11},... | collective-permute-start | bytes 393224 | tf_op jit(solution)/shard_map/ppermute | solution.py:12
  49.0 12.1 %collective-permute-start.10 = (bf16[128,4,128]{2,0,1:T(8,128)(2,1)S(1)}, bf16[128,4,128]{2,0,1:T(8,128)(2,1)S(1)}, u32[]{:S(2)}, u32[]{:S(2)}) collective-permute-start(bf16[128,4,128]{2,0,1:T(8,128)(2,1)S(1)} %fusion.40), channel_id=1, source_target_pairs={{3,0},{4,1},{5,2},{6,3},{7,4},{11,8},{12,9},{13,10},{14,11},{15,12... | collective-permute-start | bytes 393224 | tf_op jit(solution)/shard_map/ppermute | solution.py:12
  53.2 14.2 %collective-permute-start.11 = (bf16[128,4,128]{2,0,1:T(8,128)(2,1)S(1)}, bf16[128,4,128]{2,0,1:T(8,128)(2,1)S(1)}, u32[]{:S(2)}, u32[]{:S(2)}) collective-permute-start(bf16[128,4,128]{2,0,1:T(8,128)(2,1)S(1)} %fusion.39), channel_id=1, source_target_pairs={{4,0},{5,1},{6,2},{7,3},{12,8},{13,9},{14,10},{15,11},{20,16},{21,... | collective-permute-start | bytes 393224 | tf_op jit(solution)/shard_map/ppermute | solution.py:12
  58.5 11.4 %collective-permute-start.13 = (bf16[128,4,128]{2,0,1:T(8,128)(2,1)S(1)}, bf16[128,4,128]{2,0,1:T(8,128)(2,1)S(1)}, u32[]{:S(2)}, u32[]{:S(2)}) collective-permute-start(bf16[128,4,128]{2,0,1:T(8,128)(2,1)S(1)} %fusion.45), channel_id=1, source_target_pairs={{2,0},{3,1},{4,2},{5,3},{6,4},{7,5},{10,8},{11,9},{12,10},{13,11},... | collective-permute-start | bytes 393224 | tf_op jit(solution)/shard_map/ppermute | solution.py:12
  59.8 12.2 %collective-permute-start.14 = (bf16[128,4,128]{2,0,1:T(8,128)(2,1)S(1)}, bf16[128,4,128]{2,0,1:T(8,128)(2,1)S(1)}, u32[]{:S(2)}, u32[]{:S(2)}) collective-permute-start(bf16[128,4,128]{2,0,1:T(8,128)(2,1)S(1)} %fusion.44), channel_id=1, source_target_pairs={{3,0},{4,1},{5,2},{6,3},{7,4},{11,8},{12,9},{13,10},{14,11},{15,12... | collective-permute-start | bytes 393224 | tf_op jit(solution)/shard_map/ppermute | solution.py:12
  61.1 19.1 %collective-permute-start.15 = (bf16[128,4,128]{2,0,1:T(8,128)(2,1)S(1)}, bf16[128,4,128]{2,0,1:T(8,128)(2,1)S(1)}, u32[]{:S(2)}, u32[]{:S(2)}) collective-permute-start(bf16[128,4,128]{2,0,1:T(8,128)(2,1)S(1)} %fusion.43), channel_id=1, source_target_pairs={{4,0},{5,1},{6,2},{7,3},{12,8},{13,9},{14,10},{15,11},{20,16},{21,... | collective-permute-start | bytes 393224 | tf_op jit(solution)/shard_map/ppermute | solution.py:12
where the time goes:
time: 82.1 us; the launch traced here: 81.6 us
  starting transfers between devices  37 us (45%)
  waiting for transfers between devices  19.6 us (24%)
  matrix products  15.9 us (19%)
  local copies, waits for them, and re-layouts  5.2 us (6%)
  other arithmetic  2.62 us (3%)
  between operations  1.17 us (1%)
    ppermute x16, starting transfers between devices, from_behind(): lax.ppermute(value, axis, [(source, source + steps) for source in range(i...  37 us
    ppermute x16, waiting for transfers between devices, from_behind(): lax.ppermute(value, axis, [(source, source + steps) for source in range(i...  19.6 us
    unnamed x17, local copies, waits for them, and re-layouts  5.14 us
    dot_general x5, matrix products, gradients(): jnp.einsum('tkgd,skd->kgts', query_grp, key_blk, preferred_element_type=j...  3.92 us
    dot_general x5, matrix products, gradients(): jnp.einsum('tkgd,skd->kgts', grad_grp, val_blk, preferred_element_type=jn...  3.26 us
    dot_general x5, matrix products, gradients(): jnp.einsum('kgts,tkgd->skd', probs_low, grad_grp, preferred_element_type=...  2.95 us
    dot_general x5, matrix products, gradients(): jnp.einsum('kgts,tkgd->skd', dscores, query_grp, preferred_element_type=j...  2.9 us
    dot_general x5, matrix products, gradients(): jnp.einsum('kgts,skd->tkgd', dscores, key_blk, preferred_element_type=jnp...  2.88 us
  transfers between devices with their start and end apart: 16, of which 6 were waited for; matrix products, arithmetic and copies ran while one was open for 26% of the time, Pallas kernels for 0%

commit v1 on v0

v1 whole, which is shorter than its diff:
```python
import functools

import jax
import jax.numpy as jnp
from jax import lax
from jax.experimental import pallas as pl
from jax.experimental.pallas import tpu as pltpu
from jax.sharding import PartitionSpec as P

LOG2E = 1.4426950408889634
VMEM = pl.BlockSpec(memory_space=pltpu.VMEM)
SMEM = pl.BlockSpec(memory_space=pltpu.SMEM)


def params(mib):
    return pltpu.CompilerParams(vmem_limit_bytes=mib * 1024 * 1024)


def split3(value):
    high = value.astype(jnp.bfloat16).astype(jnp.float32)
    rest = value - high
    middle = rest.astype(jnp.bfloat16).astype(jnp.float32)
    return high, middle, rest - middle


def stats_kernel(heads, grad_ref, out_ref, log_ref, aux_ref):
    rows = grad_ref.shape[0]
    delta = jnp.sum(
        grad_ref[...].astype(jnp.float32) * out_ref[...].astype(jnp.float32), axis=-1, keepdims=True
    )
    d_high, d_mid, d_low = split3(delta)
    l_high, l_mid, l_low = split3(log_ref[...])
    lane_row = lax.broadcasted_iota(jnp.int32, (rows, 128), 1)
    logs = jnp.where(
        lane_row < heads, l_high, jnp.where(lane_row < 2 * heads, l_mid, l_low)
    )
    lane = lax.broadcasted_iota(jnp.int32, (1, heads, 128), 2)
    head = lax.broadcasted_iota(jnp.int32, (1, heads, 128), 1)
    own = (lane == head) | (lane == head + heads) | (lane == head + 2 * heads)
    aux = jnp.where(own, logs[:, None, :], 0.0)
    aux = jnp.where(lane == 3 * heads, d_high, aux)
    aux = jnp.where(lane == 3 * heads + 1, d_mid, aux)
    aux = jnp.where(lane == 3 * heads + 2, d_low, aux)
    aux_ref[...] = aux.astype(jnp.bfloat16)


def stats(out_grad, attn_out, logs4):
    rows, heads, size = out_grad.shape
    steps = 4
    big = pl.BlockSpec((rows // steps, heads, size), lambda i: (i, 0, 0))
    return pl.pallas_call(
        functools.partial(stats_kernel, heads),
        grid=(steps,),
        in_specs=[big, big, pl.BlockSpec((rows // steps, 128), lambda i: (i, 0))],
        out_specs=big,
        out_shape=jax.ShapeDtypeStruct((rows, heads, 128), jnp.bfloat16),
        compiler_params=params(16),
        name="stats",
    )(out_grad, attn_out, logs4)


def chunk_kernel(
    scale, info_ref, end_ref, q0, g0, a0, q1, g1, a1, k_ref, v_ref, ds_ref, dk_ref, dv_ref, dk_acc, dv_acc
):
    rows, heads, size = q0.shape
    kv_count = k_ref.shape[1]
    group = heads // kv_count
    count = rows * group
    width = k_ref.shape[0]
    dk_acc[...] = jnp.zeros_like(dk_acc)
    dv_acc[...] = jnp.zeros_like(dv_acc)
    key_start = info_ref[0]
    last_end = info_ref[3]
    lane = lax.broadcasted_iota(jnp.int32, (width, 128), 1)
    log_cols = jnp.where(lane < 3 * heads, -1.0, 0.0).astype(jnp.bfloat16)
    delta_cols = jnp.where((lane >= 3 * heads) & (lane < 3 * heads + 3), -1.0, 0.0).astype(jnp.bfloat16)
    for side, (q_ref, g_ref, a_ref) in enumerate(((q0, g0, a0), (q1, g1, a1))):
        start = info_ref[1 + side]
        live = (key_start < start + rows) & (last_end >= start)

        @pl.when(live)
        def _():
            pos = start + lax.broadcasted_iota(jnp.int32, (rows, group, width), 0).reshape(count, width)
            key_pos = key_start + lax.broadcasted_iota(jnp.int32, (1, width), 1)
            mask = (pos >= key_pos) & (pos <= end_ref[...])
            for kv in range(kv_count):
                span = slice(kv * group, (kv + 1) * group)
                query = q_ref[:, span, :].reshape(count, size)
                grad = g_ref[:, span, :].reshape(count, size)
                aux = a_ref[:, span, :].reshape(count, 128)
                key = jnp.concatenate([k_ref[:, kv, :], log_cols], axis=1)
                val = jnp.concatenate([v_ref[:, kv, :], delta_cols], axis=1)
                nt = (((1,), (1,)), ((), ()))
                tn = (((0,), (0,)), ((), ()))
                logits = lax.dot_general(
                    jnp.concatenate([query, aux], axis=1), key, nt, preferred_element_type=jnp.float32
                )
                probs = jnp.where(mask, jnp.exp2(logits * (scale * LOG2E)), 0.0)
                diff = lax.dot_general(
                    jnp.concatenate([grad, aux], axis=1), val, nt, preferred_element_type=jnp.float32
                )
                ds = (probs * diff).astype(jnp.bfloat16)
                ds_ref[side, kv] = ds
                dv_acc[kv] += lax.dot_general(
                    probs.astype(jnp.bfloat16), grad, tn, preferred_element_type=jnp.float32
                )
                dk_acc[kv] += lax.dot_general(ds, query, tn, preferred_element_type=jnp.float32)

        @pl.when(jnp.logical_not(live))
        def _():
            ds_ref[side] = jnp.zeros(ds_ref.shape[1:], ds_ref.dtype)

    dk_ref[...] = (dk_acc[...] * scale).astype(dk_ref.dtype)
    dv_ref[...] = dv_acc[...].astype(dv_ref.dtype)


def chunk(scale, info, end, own, other, key, val, kind, name):
    rows, heads, size = own[0].shape
    width, kv_count = key.shape[:2]
    group = heads // kv_count
    acc = (kv_count, width, size)
    return pl.pallas_call(
        functools.partial(chunk_kernel, scale),
        in_specs=[SMEM] + [VMEM] * 9,
        out_specs=[VMEM] * 3,
        out_shape=[
            jax.ShapeDtypeStruct((2, kv_count, rows * group, width), jnp.bfloat16),
            jax.ShapeDtypeStruct(acc, kind),
            jax.ShapeDtypeStruct(acc, kind),
        ],
        scratch_shapes=[pltpu.VMEM(acc, jnp.float32), pltpu.VMEM(acc, jnp.float32)],
        compiler_params=params(32),
        name=name,
    )(info, end, *own, *other, key, val)


def query_kernel(scale, side, add, ds0, ds1, ds2, k0, k1, k2, *rest):
    out_ref = rest[-1]
    rows, heads, size = out_ref.shape
    kv_count = k0.shape[1]
    group = heads // kv_count
    for kv in range(kv_count):
        ds = jnp.concatenate([ds0[side, kv], ds1[side, kv], ds2[side, kv]], axis=1)
        key = jnp.concatenate([k0[:, kv, :], k1[:, kv, :], k2[:, kv, :]], axis=0)
        total = jnp.dot(ds, key, preferred_element_type=jnp.float32) * scale
        total = total.reshape(rows, group, size)
        span = slice(kv * group, (kv + 1) * group)
        if add:
            total = total + rest[0][:, span, :].astype(jnp.float32)
        out_ref[:, span, :] = total.astype(out_ref.dtype)


def query_grads(scale, side, ds, key, more, shape, name):
    return pl.pallas_call(
        functools.partial(query_kernel, scale, side, bool(more)),
        in_specs=[VMEM] * (6 + len(more)),
        out_specs=VMEM,
        out_shape=jax.ShapeDtypeStruct(shape, jnp.bfloat16),
        compiler_params=params(32),
        name=name,
    )(*ds, *key, *more)


def on_device(queries, keys, values, attn_out, out_grad, log_sums, doc_ids):
    width, heads, head_size = queries.shape
    scale = head_size ** (-0.5)
    count = lax.axis_size("seq")
    shard = lax.axis_index("seq")
    other = shard ^ 1

    def flip(value):
        return lax.ppermute(value, "seq", [(i, i ^ 1) for i in range(count)])

    def move(value, steps):
        return lax.ppermute(
            value, "seq", [(i, i + steps) for i in range(count) if 0 <= i + steps < count]
        )

    query_other, grad_other = flip(queries), flip(out_grad)
    key1, val1 = move(keys, 2), move(values, 2)
    key2, val2 = move(keys, 4), move(values, 4)
    logs4 = jnp.tile(log_sums.T * (head_size**0.5), (1, 128 // heads))
    aux = stats(out_grad, attn_out, logs4)
    aux_other = flip(aux)

    def bounds(distance):
        start = (shard - distance) * width
        docs = lax.dynamic_slice_in_dim(doc_ids, jnp.maximum(start, 0), width, 0)
        end = jnp.sum(doc_ids[None, :] <= docs[:, None], axis=1, dtype=jnp.int32) - 1
        end = jnp.where(start < 0, -1, end)
        info = jnp.stack([start, shard * width, other * width, end[-1]])
        return info, end[None, :]

    own = (queries, out_grad, aux)
    far = (query_other, grad_other, aux_other)
    ds0, dk0, dv0 = chunk(scale, *bounds(0), own, far, keys, values, jnp.float32, "chunk0")
    ds1, dk1, dv1 = chunk(scale, *bounds(2), own, far, key1, val1, jnp.bfloat16, "chunk1")
    dv1, dk1 = move(dv1, -2), move(dk1, -2)
    ds2, dk2, dv2 = chunk(scale, *bounds(4), own, far, key2, val2, jnp.bfloat16, "chunk2")
    dv2, dk2 = move(dv2, -4), move(dk2, -4)
    ds, ks = (ds0, ds1, ds2), (keys, key1, key2)
    part = query_grads(scale, 1, ds, ks, (), queries.shape, "query_other")
    query_grad = query_grads(scale, 0, ds, ks, (flip(part),), queries.shape, "query_own")

    def total(first, *rest):
        for one in rest:
            first = first + one.astype(jnp.float32)
        return first.astype(jnp.bfloat16).transpose(1, 0, 2)

    return query_grad, total(dk0, dk1, dk2), total(dv0, dv1, dv2)


def solution(mesh):
    rows = P(("dp", "seq"), None, None)
    return jax.shard_map(
        on_device,
        mesh=mesh,
        in_specs=(rows,) * 5 + (P(None, ("dp", "seq")), P("dp")),
        out_specs=(rows,) * 3,
        check_vma=False,
    )
```

time: 82.1 us -> 61.8 us (0.75)
  the two profiles are of different devices: /device:TPU:0 before, /device:TPU:15 now
where the time goes in v1:
time: 61.8 us; the launch traced here: 61.4 us
  starting transfers between devices  20.4 us (33%)
  Pallas kernels  18.3 us (30%)
  waiting for transfers between devices  12.3 us (20%)
  local copies, waits for them, and re-layouts  6.14 us (10%)
  other arithmetic  3.36 us (5%)
  between operations  0.88 us (1%)
    ppermute x8, starting transfers between devices, move(): lax.ppermute(value, 'seq', [(i, i + steps) for i in range(count) if 0 <=...  16.5 us
    pallas_call x3, Pallas kernels, chunk(): pl.pallas_call(functools.partial(chunk_kernel, scale), in_specs=[SMEM] +...  13.4 us
    ppermute x8, waiting for transfers between devices, move(): lax.ppermute(value, 'seq', [(i, i + steps) for i in range(count) if 0 <=...  12.2 us
    unnamed x16, local copies, waits for them, and re-layouts  4.07 us
    ppermute x4, starting transfers between devices, flip(): return lax.ppermute(value, 'seq', [(i, i ^ 1) for i in range(count)])  3.88 us
    pallas_call x2, Pallas kernels, query_grads(): pl.pallas_call(functools.partial(query_kernel, scale, side, bool(more)),...  3.81 us
    another operation x3, other arithmetic, bounds(): info = jnp.stack([start, shard * width, other * width, end[-1]])  2.19 us
    slice x3, local copies, waits for them, and re-layouts, bounds(): info = jnp.stack([start, shard * width, other * width, end[-1]])  1.89 us
  transfers between devices with their start and end apart: 12, of which 4 were waited for; matrix products, arithmetic and copies ran while one was open for 11% of the time, Pallas kernels for 13%

profile of v1, /device:TPU:15, one launch (start us, length us, event | category | flops | bytes accessed | tf_op | source)
XLA Modules:
  0.0 61.4 jit_solution(10263125000443532743)
XLA Ops:
  0.6 0.0 copy-start.6
  0.6 0.0 copy-start.3
  0.7 5.0 %collective-permute-start.6 = (bf16[128,4,128]{2,1,0:T(4,128)(2,1)}, bf16[128,4,128]{2,1,0:T(4,128)(2,1)}, u32[]{:S(2)}, u32[]{:S(2)}) collective-permute-start(bf16[128,4,128]{2,1,0:T(4,128)(2,1)} %v_ref.1), channel_id=1, source_target_pairs={{0,4},{1,5},{2,6},{3,7},{8,12},{9,13},{10,14},{11,15},{16,20},{17,... | collective-permute-start | bytes 393224 | tf_op jit(solution)/shard_map/ppermute | solution.py:175
  5.7 1.9 %collective-permute-start.4 = (bf16[128,4,128]{2,1,0:T(4,128)(2,1)}, bf16[128,4,128]{2,1,0:T(4,128)(2,1)}, u32[]{:S(2)}, u32[]{:S(2)}) collective-permute-start(bf16[128,4,128]{2,1,0:T(4,128)(2,1)} %v_ref.1), channel_id=1, source_target_pairs={{0,2},{1,3},{2,4},{3,5},{4,6},{5,7},{8,10},{9,11},{10,12},{11,13},... | collective-permute-start | bytes 393224 | tf_op jit(solution)/shard_map/ppermute | solution.py:175
  7.6 1.0 %collective-permute-start.1 = (bf16[128,32,128]{2,1,0:T(8,128)(2,1)}, bf16[128,32,128]{2,1,0:T(8,128)(2,1)}, u32[]{:S(2)}, u32[]{:S(2)}) collective-permute-start(bf16[128,32,128]{2,1,0:T(8,128)(2,1)} %g0.5), channel_id=1, source_target_pairs={{0,1},{1,0},{2,3},{3,2},{4,5},{5,4},{6,7},{7,6},{8,9},{9,8},{10,11... | collective-permute-start | bytes 3145736 | tf_op jit(solution)/shard_map/ppermute | solution.py:172
  8.6 0.7 %multiply_bitcast_fusion = f32[128,32]{0,1:T(8,128)S(1)} fusion(f32[32,128]{1,0:T(8,128)} %param.12), kind=kLoop, calls=%fused_computation.7 | loop fusion | flops 4096 | bytes 32768 | tf_op jit(solution)/shard_map/mul | solution.py:182
  9.3 0.1 copy.16.log_ref
  9.4 0.0 copy-start
  9.4 1.2 %copy-done = bf16[128,32,128]{2,1,0:T(8,128)(2,1)S(1)} copy-done((bf16[128,32,128]{2,1,0:T(8,128)(2,1)S(1)}, bf16[128,32,128]{2,1,0:T(8,128)(2,1)}, u32[]{:S(2)}) %copy-start) | copy-done | bytes 1048600
  10.6 0.0 copy-start.4
  10.7 1.2 %copy-done.4 = bf16[128,32,128]{2,1,0:T(8,128)(2,1)S(1)} copy-done((bf16[128,32,128]{2,1,0:T(8,128)(2,1)S(1)}, bf16[128,32,128]{2,1,0:T(8,128)(2,1)}, u32[]{:S(2)}) %copy-start.4) | copy-done | bytes 1048600
  11.9 0.0 copy-start.2
  11.9 0.0 copy-start.1
  11.9 0.0 copy-start.5
  11.9 1.0 %stats.1.a0 = bf16[128,32,128]{2,1,0:T(8,128)(2,1)S(1)} custom-call(bf16[128,32,128]{2,1,0:T(8,128)(2,1)S(1)} %copy-done, bf16[128,32,128]{2,1,0:T(8,128)(2,1)S(1)} %copy-done.4, f32[128,128]{1,0:T(8,128)S(1)} %copy.16.log_ref), custom_call_target="tpu_custom_call" | custom-call | tf_op jit(solution)/shard_map/stats/pallas_call | solution.py:51
  12.9 0.1 collective-permute-start.2
  13.0 0.1 copy-done.2
  13.1 0.4 collective-permute-start
  13.5 0.0 copy-done.6
  13.5 0.1 fusion.2
  13.6 0.3 convert_reduce_fusion
  13.9 0.7 %slice.11 = s32[1]{0:T(128)} slice(s32[128]{0:T(128)S(1)} %broadcast_select_fusion), slice={[127:128]} | slice | bytes 8 | tf_op jit(solution)/shard_map/slice | solution.py:191
  14.6 0.6 %slice.9 = s32[1]{0:T(128)} slice(s32[128]{0:T(128)S(1)} %broadcast_select_fusion.2), slice={[127:128]} | slice | bytes 8 | tf_op jit(solution)/shard_map/slice | solution.py:191
  15.3 0.7 %pad_add_fusion.info_ref = s32[4]{0:T(128)S(1)} fusion(s32[1]{0:T(128)} %slice.9, s32[1]{0:T(128)} %bitcast, s32[1]{0:T(128)} %bitcast.1), kind=kLoop, calls=%fused_computation.11 | loop fusion | flops 12 | bytes 28 | tf_op jit(solution)/shard_map/stack | solution.py:191
  16.0 0.0 collective-permute-done.2.a1
  16.0 0.0 copy-done.3
  16.0 1.3 %collective-permute-start.5 = (bf16[128,4,128]{2,1,0:T(4,128)(2,1)S(1)}, bf16[128,4,128]{2,1,0:T(4,128)(2,1)S(1)}, u32[]{:S(2)}, u32[]{:S(2)}) collective-permute-start(bf16[128,4,128]{2,1,0:T(4,128)(2,1)S(1)} %copy-done.3), channel_id=1, source_target_pairs={{0,4},{1,5},{2,6},{3,7},{8,12},{9,13},{10,14},{11,15},{16,20},{17,... | collective-permute-start | bytes 393224 | tf_op jit(solution)/shard_map/ppermute | solution.py:175
  17.3 0.0 collective-permute-done.q1
  17.3 1.9 %collective-permute-start.3 = (bf16[128,4,128]{2,1,0:T(4,128)(2,1)S(1)}, bf16[128,4,128]{2,1,0:T(4,128)(2,1)S(1)}, u32[]{:S(2)}, u32[]{:S(2)}) collective-permute-start(bf16[128,4,128]{2,1,0:T(4,128)(2,1)S(1)} %copy-done.3), channel_id=1, source_target_pairs={{0,2},{1,3},{2,4},{3,5},{4,6},{5,7},{8,10},{9,11},{10,12},{11,13},... | collective-permute-start | bytes 393224 | tf_op jit(solution)/shard_map/ppermute | solution.py:175
  19.3 0.8 %pad_add_fusion.2.info_ref = s32[4]{0:T(128)S(1)} fusion(s32[1]{0:T(128)} %slice.11, s32[1]{0:T(128)} %bitcast.7, s32[1]{0:T(128)} %bitcast.1, s32[1]{0:T(128)} %bitcast), kind=kLoop, calls=%fused_computation.13 | loop fusion | flops 12 | bytes 32 | tf_op jit(solution)/shard_map/stack | solution.py:191
  20.0 0.6 slice.10
  20.6 0.7 %pad_add_fusion.1.info_ref = s32[4]{0:T(128)S(1)} fusion(s32[1]{0:T(128)} %slice.10, s32[1]{0:T(128)} %bitcast.5, s32[1]{0:T(128)} %bitcast.1, s32[1]{0:T(128)} %bitcast), kind=kLoop, calls=%fused_computation.12 | loop fusion | flops 12 | bytes 32 | tf_op jit(solution)/shard_map/stack | solution.py:191
  21.3 0.0 collective-permute-done.1.g1
  21.3 0.0 copy-done.1
  21.3 0.0 copy-done.5
  21.3 4.4 %chunk0.1 = (bf16[2,4,1024,128]{3,2,1,0:T(8,128)(2,1)S(1)}, f32[4,128,128]{2,1,0:T(8,128)S(1)}, f32[4,128,128]{2,1,0:T(8,128)S(1)}) custom-call(s32[4]{0:T(128)S(1)} %pad_add_fusion.info_ref, s32[1,128]{1,0:T(1,128)S(1)} %fusion.5.end_ref, bf16[128,32,128]{2,1,0:T(8,128)(2,1)S(1)} %copy-done.2, bf16[128,32,128]{2,1,0:T(8,128)(2,1)S(1)} %copy-done.1, ...), custom_call_target="tpu_custom_call" | custom-call | tf_op jit(solution)/shard_map/chunk0/pallas_call | solution.py:122
  25.8 0.0 collective-permute-done.6.v_ref
  25.8 0.0 collective-permute-done.5.k_ref.k2
  25.8 2.2 %chunk2.1 = (bf16[2,4,1024,128]{3,2,1,0:T(8,128)(2,1)S(1)}, bf16[4,128,128]{2,1,0:T(8,128)(2,1)S(1)}, bf16[4,128,128]{2,1,0:T(8,128)(2,1)S(1)}) custom-call(s32[4]{0:T(128)S(1)} %pad_add_fusion.2.info_ref, s32[1,128]{1,0:T(1,128)S(1)} %fusion.3.end_ref, bf16[128,32,128]{2,1,0:T(8,128)(2,1)S(1)} %copy-done.2, bf16[128,32,128]{2,1,0:T(8,128)(2,1)S(1)} %copy-done.1, ...), custom_call_target="tpu_custom_call" | custom-call | tf_op jit(solution)/shard_map/chunk2/pallas_call | solution.py:122
  28.0 0.0 collective-permute-done.4.v_ref
  28.0 0.0 collective-permute-done.3.k_ref.k1
  28.0 6.8 %chunk1.1 = (bf16[2,4,1024,128]{3,2,1,0:T(8,128)(2,1)S(1)}, bf16[4,128,128]{2,1,0:T(8,128)(2,1)S(1)}, bf16[4,128,128]{2,1,0:T(8,128)(2,1)S(1)}) custom-call(s32[4]{0:T(128)S(1)} %pad_add_fusion.1.info_ref, s32[1,128]{1,0:T(1,128)S(1)} %fusion.4.end_ref, bf16[128,32,128]{2,1,0:T(8,128)(2,1)S(1)} %copy-done.2, bf16[128,32,128]{2,1,0:T(8,128)(2,1)S(1)} %copy-done.1, ...), custom_call_target="tpu_custom_call" | custom-call | tf_op jit(solution)/shard_map/chunk1/pallas_call | solution.py:122
  34.9 1.4 %query_other.1 = bf16[128,32,128]{2,1,0:T(8,128)(2,1)S(1)} custom-call(bf16[2,4,1024,128]{3,2,1,0:T(8,128)(2,1)S(1)} %get-tuple-element.12.ds0, bf16[2,4,1024,128]{3,2,1,0:T(8,128)(2,1)S(1)} %get-tuple-element.13.ds1, bf16[2,4,1024,128]{3,2,1,0:T(8,128)(2,1)S(1)} %get-tuple-element.14.ds2, bf16[128,4,128]{2,1,0:T(4,128)(2,1)S(1)} %copy-done.3, ...), custom_call_target="tpu_custom_call" | custom-call | tf_op jit(solution)/shard_map/query_other/pallas_call | solution.py:154
  36.3 2.4 %collective-permute-start.7 = (bf16[128,32,128]{2,1,0:T(8,128)(2,1)S(1)}, bf16[128,32,128]{2,1,0:T(8,128)(2,1)S(1)}, u32[]{:S(2)}, u32[]{:S(2)}) collective-permute-start(bf16[128,32,128]{2,1,0:T(8,128)(2,1)S(1)} %query_other.1), channel_id=1, source_target_pairs={{0,1},{1,0},{2,3},{3,2},{4,5},{5,4},{6,7},{7,6},{8,9},{9,8},{10,11... | collective-permute-start | bytes 3145736 | tf_op jit(solution)/shard_map/ppermute | solution.py:172
  38.6 1.3 %collective-permute-start.9 = (bf16[4,128,128]{2,1,0:T(8,128)(2,1)S(1)}, bf16[4,128,128]{2,1,0:T(8,128)(2,1)S(1)}, u32[]{:S(2)}, u32[]{:S(2)}) collective-permute-start(bf16[4,128,128]{2,1,0:T(8,128)(2,1)S(1)} %get-tuple-element.17), channel_id=1, source_target_pairs={{4,0},{5,1},{6,2},{7,3},{12,8},{13,9},{14,10},{15,11},{20,16},{21,... | collective-permute-start | bytes 393224 | tf_op jit(solution)/shard_map/ppermute | solution.py:175
  39.9 1.9 %collective-permute-start.8 = (bf16[4,128,128]{2,1,0:T(8,128)(2,1)S(1)}, bf16[4,128,128]{2,1,0:T(8,128)(2,1)S(1)}, u32[]{:S(2)}, u32[]{:S(2)}) collective-permute-start(bf16[4,128,128]{2,1,0:T(8,128)(2,1)S(1)} %get-tuple-element.16), channel_id=1, source_target_pairs={{2,0},{3,1},{4,2},{5,3},{6,4},{7,5},{10,8},{11,9},{12,10},{13,11},... | collective-permute-start | bytes 393224 | tf_op jit(solution)/shard_map/ppermute | solution.py:175
  41.9 1.3 %collective-permute-start.11 = (bf16[4,128,128]{2,1,0:T(8,128)(2,1)S(1)}, bf16[4,128,128]{2,1,0:T(8,128)(2,1)S(1)}, u32[]{:S(2)}, u32[]{:S(2)}) collective-permute-start(bf16[4,128,128]{2,1,0:T(8,128)(2,1)S(1)} %get-tuple-element.20), channel_id=1, source_target_pairs={{4,0},{5,1},{6,2},{7,3},{12,8},{13,9},{14,10},{15,11},{20,16},{21,... | collective-permute-start | bytes 393224 | tf_op jit(solution)/shard_map/ppermute | solution.py:175
  43.2 1.9 %collective-permute-start.10 = (bf16[4,128,128]{2,1,0:T(8,128)(2,1)S(1)}, bf16[4,128,128]{2,1,0:T(8,128)(2,1)S(1)}, u32[]{:S(2)}, u32[]{:S(2)}) collective-permute-start(bf16[4,128,128]{2,1,0:T(8,128)(2,1)S(1)} %get-tuple-element.19), channel_id=1, source_target_pairs={{2,0},{3,1},{4,2},{5,3},{6,4},{7,5},{10,8},{11,9},{12,10},{13,11},... | collective-permute-start | bytes 393224 | tf_op jit(solution)/shard_map/ppermute | solution.py:175
  45.1 1.5 %collective-permute-done.9 = bf16[4,128,128]{2,1,0:T(8,128)(2,1)S(1)} collective-permute-done((bf16[4,128,128]{2,1,0:T(8,128)(2,1)S(1)}, bf16[4,128,128]{2,1,0:T(8,128)(2,1)S(1)}, u32[]{:S(2)}, u32[]{:S(2)}) %collective-permute-start.9) | collective-permute-done | bytes 131104 | tf_op jit(solution)/shard_map/ppermute | solution.py:175
  46.6 3.5 %collective-permute-done.8 = bf16[4,128,128]{2,1,0:T(8,128)(2,1)S(1)} collective-permute-done((bf16[4,128,128]{2,1,0:T(8,128)(2,1)S(1)}, bf16[4,128,128]{2,1,0:T(8,128)(2,1)S(1)}, u32[]{:S(2)}, u32[]{:S(2)}) %collective-permute-start.8) | collective-permute-done | bytes 131104 | tf_op jit(solution)/shard_map/ppermute | solution.py:175
  50.1 0.8 %copy.17 = bf16[128,4,128]{2,1,0:T(4,128)(2,1)} copy(bf16[128,4,128]{2,0,1:T(8,128)(2,1)S(1)} %fusion) | data formatting | bytes 262144
  50.8 1.4 %collective-permute-done.11 = bf16[4,128,128]{2,1,0:T(8,128)(2,1)S(1)} collective-permute-done((bf16[4,128,128]{2,1,0:T(8,128)(2,1)S(1)}, bf16[4,128,128]{2,1,0:T(8,128)(2,1)S(1)}, u32[]{:S(2)}, u32[]{:S(2)}) %collective-permute-start.11) | collective-permute-done | bytes 131104 | tf_op jit(solution)/shard_map/ppermute | solution.py:175
  52.2 5.9 %collective-permute-done.10 = bf16[4,128,128]{2,1,0:T(8,128)(2,1)S(1)} collective-permute-done((bf16[4,128,128]{2,1,0:T(8,128)(2,1)S(1)}, bf16[4,128,128]{2,1,0:T(8,128)(2,1)S(1)}, u32[]{:S(2)}, u32[]{:S(2)}) %collective-permute-start.10) | collective-permute-done | bytes 131104 | tf_op jit(solution)/shard_map/ppermute | solution.py:175
  58.1 0.1 fusion.1
  58.2 0.8 %copy.18 = bf16[128,4,128]{2,1,0:T(4,128)(2,1)} copy(bf16[128,4,128]{2,0,1:T(8,128)(2,1)S(1)} %fusion.1) | data formatting | bytes 262144
  58.9 0.0 collective-permute-done.7.rest_0_
  58.9 2.4 %query_own.1 = bf16[128,32,128]{2,1,0:T(8,128)(2,1)} custom-call(bf16[2,4,1024,128]{3,2,1,0:T(8,128)(2,1)S(1)} %get-tuple-element.12.ds0, bf16[2,4,1024,128]{3,2,1,0:T(8,128)(2,1)S(1)} %get-tuple-element.13.ds1, bf16[2,4,1024,128]{3,2,1,0:T(8,128)(2,1)S(1)} %get-tuple-element.14.ds2, bf16[128,4,128]{2,1,0:T(4,128)(2,1)S(1)} %copy-done.3, ...), custom_call_target="tpu_custom_call" | custom-call | tf_op jit(solution)/shard_map/query_own/pallas_call | solution.py:154
  (8 shorter events, 0.1 us)
Async XLA Ops:
  0.6 12.9 %copy-start.6 = (s32[1024]{0:T(1024)S(1)}, s32[1024]{0:T(1024)}, u32[]{:S(2)}) copy-start(s32[1024]{0:T(1024)} %param.13) | copy-start | bytes 12292
  0.6 15.4 %copy-start.3 = (bf16[128,4,128]{2,1,0:T(4,128)(2,1)S(1)}, bf16[128,4,128]{2,1,0:T(4,128)(2,1)}, u32[]{:S(2)}) copy-start(bf16[128,4,128]{2,1,0:T(4,128)(2,1)} %k0.3) | copy-start | bytes 393220
  0.7 25.1 %collective-permute-start.6 = (bf16[128,4,128]{2,1,0:T(4,128)(2,1)}, bf16[128,4,128]{2,1,0:T(4,128)(2,1)}, u32[]{:S(2)}, u32[]{:S(2)}) collective-permute-start(bf16[128,4,128]{2,1,0:T(4,128)(2,1)} %v_ref.1), channel_id=1, source_target_pairs={{0,4},{1,5},{2,6},{3,7},{8,12},{9,13},{10,14},{11,15},{16,20},{17,... | collective-permute-start | bytes 393224 | tf_op jit(solution)/shard_map/ppermute | solution.py:175
  5.7 22.4 %collective-permute-start.4 = (bf16[128,4,128]{2,1,0:T(4,128)(2,1)}, bf16[128,4,128]{2,1,0:T(4,128)(2,1)}, u32[]{:S(2)}, u32[]{:S(2)}) collective-permute-start(bf16[128,4,128]{2,1,0:T(4,128)(2,1)} %v_ref.1), channel_id=1, source_target_pairs={{0,2},{1,3},{2,4},{3,5},{4,6},{5,7},{8,10},{9,11},{10,12},{11,13},... | collective-permute-start | bytes 393224 | tf_op jit(solution)/shard_map/ppermute | solution.py:175
  7.6 13.8 %collective-permute-start.1 = (bf16[128,32,128]{2,1,0:T(8,128)(2,1)}, bf16[128,32,128]{2,1,0:T(8,128)(2,1)}, u32[]{:S(2)}, u32[]{:S(2)}) collective-permute-start(bf16[128,32,128]{2,1,0:T(8,128)(2,1)} %g0.5), channel_id=1, source_target_pairs={{0,1},{1,0},{2,3},{3,2},{4,5},{5,4},{6,7},{7,6},{8,9},{9,8},{10,11... | collective-permute-start | bytes 3145736 | tf_op jit(solution)/shard_map/ppermute | solution.py:172
  9.4 1.2 %copy-start = (bf16[128,32,128]{2,1,0:T(8,128)(2,1)S(1)}, bf16[128,32,128]{2,1,0:T(8,128)(2,1)}, u32[]{:S(2)}) copy-start(bf16[128,32,128]{2,1,0:T(8,128)(2,1)} %g0.5) | copy-start | bytes 3145732
  10.6 1.2 %copy-start.4 = (bf16[128,32,128]{2,1,0:T(8,128)(2,1)S(1)}, bf16[128,32,128]{2,1,0:T(8,128)(2,1)}, u32[]{:S(2)}) copy-start(bf16[128,32,128]{2,1,0:T(8,128)(2,1)} %out_ref.1) | copy-start | bytes 3145732
  11.9 1.2 %copy-start.2 = (bf16[128,32,128]{2,1,0:T(8,128)(2,1)S(1)}, bf16[128,32,128]{2,1,0:T(8,128)(2,1)}, u32[]{:S(2)}) copy-start(bf16[128,32,128]{2,1,0:T(8,128)(2,1)} %q0.5) | copy-start | bytes 3145732
  11.9 9.5 %copy-start.1 = (bf16[128,32,128]{2,1,0:T(8,128)(2,1)S(1)}, bf16[128,32,128]{2,1,0:T(8,128)(2,1)}, u32[]{:S(2)}) copy-start(bf16[128,32,128]{2,1,0:T(8,128)(2,1)} %g0.5) | copy-start | bytes 3145732
  11.9 9.5 %copy-start.5 = (bf16[128,4,128]{2,1,0:T(4,128)(2,1)S(1)}, bf16[128,4,128]{2,1,0:T(4,128)(2,1)}, u32[]{:S(2)}) copy-start(bf16[128,4,128]{2,1,0:T(4,128)(2,1)} %v_ref.1) | copy-start | bytes 393220
  12.9 3.1 %collective-permute-start.2 = (bf16[128,32,128]{2,1,0:T(8,128)(2,1)S(1)}, bf16[128,32,128]{2,1,0:T(8,128)(2,1)}, u32[]{:S(2)}, u32[]{:S(2)}) collective-permute-start(bf16[128,32,128]{2,1,0:T(8,128)(2,1)S(1)} %stats.1.a0), channel_id=1, source_target_pairs={{0,1},{1,0},{2,3},{3,2},{4,5},{5,4},{6,7},{7,6},{8,9},{9,8},{10,11... | collective-permute-start | bytes 3145736 | tf_op jit(solution)/shard_map/ppermute | solution.py:172
  13.1 4.2 %collective-permute-start = (bf16[128,32,128]{2,1,0:T(8,128)(2,1)S(1)}, bf16[128,32,128]{2,1,0:T(8,128)(2,1)}, u32[]{:S(2)}, u32[]{:S(2)}) collective-permute-start(bf16[128,32,128]{2,1,0:T(8,128)(2,1)S(1)} %copy-done.2), channel_id=1, source_target_pairs={{0,1},{1,0},{2,3},{3,2},{4,5},{5,4},{6,7},{7,6},{8,9},{9,8},{10,11... | collective-permute-start | bytes 3145736 | tf_op jit(solution)/shard_map/ppermute | solution.py:172
  16.0 9.8 %collective-permute-start.5 = (bf16[128,4,128]{2,1,0:T(4,128)(2,1)S(1)}, bf16[128,4,128]{2,1,0:T(4,128)(2,1)S(1)}, u32[]{:S(2)}, u32[]{:S(2)}) collective-permute-start(bf16[128,4,128]{2,1,0:T(4,128)(2,1)S(1)} %copy-done.3), channel_id=1, source_target_pairs={{0,4},{1,5},{2,6},{3,7},{8,12},{9,13},{10,14},{11,15},{16,20},{17,... | collective-permute-start | bytes 393224 | tf_op jit(solution)/shard_map/ppermute | solution.py:175
  17.3 10.7 %collective-permute-start.3 = (bf16[128,4,128]{2,1,0:T(4,128)(2,1)S(1)}, bf16[128,4,128]{2,1,0:T(4,128)(2,1)S(1)}, u32[]{:S(2)}, u32[]{:S(2)}) collective-permute-start(bf16[128,4,128]{2,1,0:T(4,128)(2,1)S(1)} %copy-done.3), channel_id=1, source_target_pairs={{0,2},{1,3},{2,4},{3,5},{4,6},{5,7},{8,10},{9,11},{10,12},{11,13},... | collective-permute-start | bytes 393224 | tf_op jit(solution)/shard_map/ppermute | solution.py:175
  36.3 22.7 %collective-permute-start.7 = (bf16[128,32,128]{2,1,0:T(8,128)(2,1)S(1)}, bf16[128,32,128]{2,1,0:T(8,128)(2,1)S(1)}, u32[]{:S(2)}, u32[]{:S(2)}) collective-permute-start(bf16[128,32,128]{2,1,0:T(8,128)(2,1)S(1)} %query_other.1), channel_id=1, source_target_pairs={{0,1},{1,0},{2,3},{3,2},{4,5},{5,4},{6,7},{7,6},{8,9},{9,8},{10,11... | collective-permute-start | bytes 3145736 | tf_op jit(solution)/shard_map/ppermute | solution.py:172
  38.6 7.9 %collective-permute-start.9 = (bf16[4,128,128]{2,1,0:T(8,128)(2,1)S(1)}, bf16[4,128,128]{2,1,0:T(8,128)(2,1)S(1)}, u32[]{:S(2)}, u32[]{:S(2)}) collective-permute-start(bf16[4,128,128]{2,1,0:T(8,128)(2,1)S(1)} %get-tuple-element.17), channel_id=1, source_target_pairs={{4,0},{5,1},{6,2},{7,3},{12,8},{13,9},{14,10},{15,11},{20,16},{21,... | collective-permute-start | bytes 393224 | tf_op jit(solution)/shard_map/ppermute | solution.py:175
  39.9 10.1 %collective-permute-start.8 = (bf16[4,128,128]{2,1,0:T(8,128)(2,1)S(1)}, bf16[4,128,128]{2,1,0:T(8,128)(2,1)S(1)}, u32[]{:S(2)}, u32[]{:S(2)}) collective-permute-start(bf16[4,128,128]{2,1,0:T(8,128)(2,1)S(1)} %get-tuple-element.16), channel_id=1, source_target_pairs={{2,0},{3,1},{4,2},{5,3},{6,4},{7,5},{10,8},{11,9},{12,10},{13,11},... | collective-permute-start | bytes 393224 | tf_op jit(solution)/shard_map/ppermute | solution.py:175
  41.9 10.4 %collective-permute-start.11 = (bf16[4,128,128]{2,1,0:T(8,128)(2,1)S(1)}, bf16[4,128,128]{2,1,0:T(8,128)(2,1)S(1)}, u32[]{:S(2)}, u32[]{:S(2)}) collective-permute-start(bf16[4,128,128]{2,1,0:T(8,128)(2,1)S(1)} %get-tuple-element.20), channel_id=1, source_target_pairs={{4,0},{5,1},{6,2},{7,3},{12,8},{13,9},{14,10},{15,11},{20,16},{21,... | collective-permute-start | bytes 393224 | tf_op jit(solution)/shard_map/ppermute | solution.py:175
  43.2 15.0 %collective-permute-start.10 = (bf16[4,128,128]{2,1,0:T(8,128)(2,1)S(1)}, bf16[4,128,128]{2,1,0:T(8,128)(2,1)S(1)}, u32[]{:S(2)}, u32[]{:S(2)}) collective-permute-start(bf16[4,128,128]{2,1,0:T(8,128)(2,1)S(1)} %get-tuple-element.19), channel_id=1, source_target_pairs={{2,0},{3,1},{4,2},{5,3},{6,4},{7,5},{10,8},{11,9},{12,10},{13,11},... | collective-permute-start | bytes 393224 | tf_op jit(solution)/shard_map/ppermute | solution.py:175

commit v2 on v0

v2 whole, which is shorter than its diff:
```python
import functools

import jax
import jax.numpy as jnp
from jax import lax
from jax.experimental import pallas as pl
from jax.experimental.pallas import tpu as pltpu
from jax.sharding import PartitionSpec as P

COSTS = {
    "pack": 10,
    "prep": 10,
    "mid": 10,
    "far0": 10,
    "far1": 10,
    "near": 10,
    "query_other": 1,
    "query_own": 10,
    "sums": 10,
}
LOG2E = 1.4426950408889634
HBM = pl.BlockSpec(memory_space=pltpu.HBM)
VMEM = pl.BlockSpec(memory_space=pltpu.VMEM)
NT = (((1,), (1,)), ((), ()))
TN = (((0,), (0,)), ((), ()))
BF = jnp.bfloat16
F32 = jnp.float32


def call(kernel, name, shapes, operands, specs=None, scratch=(), after=(), mib=8):
    count = len(operands)

    def run(*refs):
        kernel(*refs[:count], *refs[count + len(after) :])

    return pl.pallas_call(
        run,
        in_specs=(specs or [VMEM] * count) + [VMEM] * len(after),
        out_specs=[VMEM] * len(shapes),
        out_shape=[jax.ShapeDtypeStruct(*one) for one in shapes],
        scratch_shapes=scratch,
        compiler_params=pltpu.CompilerParams(vmem_limit_bytes=mib * 1024 * 1024),
        cost_estimate=pl.CostEstimate(flops=int(COSTS[name] * 1e9), bytes_accessed=10**7, transcendentals=0),
        name=name,
    )(*operands, *after)


def split3(value):
    high = value.astype(BF).astype(F32)
    rest = value - high
    middle = rest.astype(BF).astype(F32)
    return high, middle, rest - middle


def start_copies(pairs, sems):
    copies = []
    for i, (source, target) in enumerate(pairs):
        copies.append(pltpu.make_async_copy(source, target, sems.at[i]))
        copies[-1].start()
    return copies


def pack_kernel(k_hbm, v_hbm, all_ref, k_ref, v_ref, sems):
    copies = start_copies(((k_hbm, k_ref), (v_hbm, v_ref)), sems)
    kv_count = k_ref.shape[1]
    for i, ref in enumerate((k_ref, v_ref)):
        copies[i].wait()
        for kv in range(kv_count):
            all_ref[i * kv_count + kv] = ref[:, kv, :]


def prep_kernel(halves, q_hbm, g_hbm, o_hbm, log_hbm, q1_ref, g1_ref, o1_ref, log1_ref, kv_ref, *refs):
    half_refs, (rows_ref, sub_ref, q_ref, g_ref, o_ref, log_ref, log_sem, sems) = refs[:halves], refs[halves:]
    rows, heads, size = q_ref.shape
    kv_count = rows_ref.shape[2]
    group = heads // kv_count
    each = kv_count // halves
    step = 32
    log_copy = start_copies(((log_hbm, log_ref),), log_sem)[0]
    copies = []
    for i, at in enumerate(range(0, rows, step)):
        part = pl.ds(at, step)
        pairs = [(one.at[part], two.at[part]) for one, two in ((g_hbm, g_ref), (o_hbm, o_ref), (q_hbm, q_ref))]
        copies.append(start_copies(pairs, sems.at[i]))
    for i, ref in enumerate(half_refs):
        ref[:each] = kv_ref[i * each : (i + 1) * each]
        ref[each:] = kv_ref[kv_count + i * each : kv_count + (i + 1) * each]
    lane_row = lax.broadcasted_iota(jnp.int32, (rows, 128), 1)
    lane = lax.broadcasted_iota(jnp.int32, (1, heads, 128), 2)
    head = lax.broadcasted_iota(jnp.int32, (1, heads, 128), 1)
    own = (lane == head) | (lane == head + heads) | (lane == head + 2 * heads)
    ones = jnp.where(lax.broadcasted_iota(jnp.int32, (128, 128), 0) < 3 * heads, 1.0, 0.0).astype(BF)
    for side, (q_one, g_one, o_one, log_one) in (
        (1, (q1_ref, g1_ref, o1_ref, log1_ref)),
        (0, (q_ref, g_ref, o_ref, log_ref)),
    ):
        if side == 0:
            log_copy.wait()
        logs = jnp.concatenate([log_one[...] * LOG2E] * (128 // heads), axis=0).T
        l_high, l_mid, l_low = split3(logs)
        logs = jnp.where(lane_row < heads, l_high, jnp.where(lane_row < 2 * heads, l_mid, l_low))
        for i, at in enumerate(range(0, rows, step)):
            part = slice(at, at + step)
            if side == 0:
                for one in copies[i]:
                    one.wait()
            grad, query = g_one[part], q_one[part]
            delta = jnp.sum(grad.astype(F32) * o_one[part].astype(F32), axis=-1, keepdims=True)
            delta = jnp.broadcast_to(delta, (step, heads, 128))
            aux = jnp.where(own, logs[part, None, :], 0.0).astype(BF)
            spot = slice(at * group, (at + step) * group)
            for kv in range(kv_count):
                span = slice(kv * group, (kv + 1) * group)
                rows_ref[side, 0, kv, spot] = query[:, span, :].reshape(step * group, size)
                rows_ref[side, 1, kv, spot] = grad[:, span, :].reshape(step * group, size)
                sub_ref[side, 0, kv, spot] = jnp.dot(
                    aux[:, span, :].reshape(step * group, 128), ones, preferred_element_type=F32
                )
                sub_ref[side, 1, kv, spot] = delta[:, span, :].reshape(step * group, 128)


def chunk_kernel(distance, first, doc_ref, rows_ref, sub_ref, kv_ref, ds_ref, out_ref, acc):
    count, size = rows_ref.shape[3:]
    each, width = kv_ref.shape[0] // 2, kv_ref.shape[1]
    rows = width
    scale = size ** (-0.5)
    shard = lax.axis_index("seq")
    key_shard = shard - distance
    key_doc = doc_ref[pl.ds(jnp.maximum(key_shard, 0), 1), :]
    acc[...] = jnp.zeros_like(acc)
    for side in range(2):
        query_shard = shard ^ side
        query_rows = jnp.broadcast_to(doc_ref[pl.ds(query_shard, 1), :], (rows, rows)).T
        ends = jnp.sum((query_rows <= key_doc).astype(jnp.int32), axis=0, keepdims=True)
        live = (key_shard >= 0) & (key_shard <= query_shard) & (jnp.max(ends) > 0)

        @pl.when(live)
        def _():
            pos = lax.broadcasted_iota(jnp.int32, (rows, count // rows, width), 0).reshape(count, width)
            low = (key_shard - query_shard) * width + lax.broadcasted_iota(jnp.int32, (1, width), 1)
            mask = (pos >= low) & (pos < ends)
            for j in range(each):
                query, grad = rows_ref[side, 0, first + j], rows_ref[side, 1, first + j]
                logits = lax.dot_general(query, kv_ref[j], NT, preferred_element_type=F32)
                logits = logits * (scale * LOG2E) - sub_ref[side, 0, first + j]
                probs = jnp.where(mask, jnp.exp2(logits), 0.0)
                diff = lax.dot_general(grad, kv_ref[each + j], NT, preferred_element_type=F32)
                ds = (probs * (diff - sub_ref[side, 1, first + j])).astype(BF)
                ds_ref[side, j] = ds
                sums = lax.dot_general(
                    jnp.concatenate([ds, probs.astype(BF)], axis=1),
                    jnp.concatenate([query, grad], axis=1),
                    TN,
                    preferred_element_type=F32,
                )
                acc[j] += sums[:width, :size] * scale
                acc[each + j] += sums[width:, size:]

        @pl.when(jnp.logical_not(live))
        def _():
            ds_ref[side] = jnp.zeros(ds_ref.shape[1:], BF)

    out_ref[...] = acc[...].astype(out_ref.dtype)


def query_kernel(side, parts, *refs):
    out_ref = refs[-1]
    total = sum(parts)
    rows, heads, size = out_ref.shape
    ds_refs, kv_refs = refs[:total], refs[total : 2 * total]
    firsts = [sum(parts[:i]) for i in range(len(parts))]
    kv_count = parts[0] * kv_refs[0].shape[0] // 2
    group = heads // kv_count

    def pick(kv, chunk):
        each = kv_count // parts[chunk]
        return firsts[chunk] + kv // each, kv % each

    for kv in range(kv_count):
        spots = [pick(kv, chunk) for chunk in range(len(parts))]
        ds = jnp.concatenate([ds_refs[i][side, j] for i, j in spots], axis=1)
        key = jnp.concatenate([kv_refs[i][j] for i, j in spots], axis=0)
        got = jnp.dot(ds, key, preferred_element_type=F32) * size ** (-0.5)
        out_ref[:, kv * group : (kv + 1) * group, :] = got.reshape(rows, group, size).astype(out_ref.dtype)


def near_kernel(parts, doc_ref, lay_ref, sub_ref, near_ref, *refs):
    rest, (ds_ref, out_ref, query_ref, acc) = refs[:-4], refs[-4:]
    chunk_kernel(0, 0, doc_ref, lay_ref, sub_ref, near_ref, ds_ref, out_ref, acc)
    more = sum(parts) - 1
    query_kernel(1, parts, ds_ref, *rest[:more], near_ref, *rest[more:], query_ref)


def sum_kernel(one_ref, two_ref, sums_ref, query_ref, key_ref, val_ref):
    query_ref[...] = (one_ref[...] + two_ref[...].astype(F32)).astype(BF)
    kv_count = key_ref.shape[1]
    for i, ref in enumerate((key_ref, val_ref)):
        heads = [sums_ref[i * kv_count + kv] for kv in range(kv_count)]
        ref[...] = jnp.stack(heads, axis=1).astype(BF)


def on_device(queries, keys, values, attn_out, out_grad, log_sums, doc_ids):
    width, heads, size = queries.shape
    kv_count = keys.shape[1]
    halves = 2
    each = kv_count // halves
    count = lax.axis_size("seq")
    docs = doc_ids.reshape(-1, width)
    rows = width * heads // kv_count
    half = (2 * each, width, size)
    full = (2 * kv_count, width, size)

    def flip(value):
        return lax.ppermute(value, "seq", [(i, i ^ 1) for i in range(count)])

    def move(value, steps):
        return lax.ppermute(
            value, "seq", [(i, i + steps) for i in range(count) if 0 <= i + steps < count]
        )

    hbm = functools.partial(pltpu.with_memory_space_constraint, memory_space=pltpu.HBM)
    (near,) = call(
        pack_kernel,
        "pack",
        [(full, BF)],
        (hbm(keys), hbm(values)),
        specs=[HBM] * 2,
        scratch=[pltpu.VMEM(keys.shape, BF)] * 2 + [pltpu.SemaphoreType.DMA((2,))],
    )
    mid = move(near, 2)
    own = (queries, out_grad, attn_out, log_sums)
    *halves_near, lay, sub = call(
        functools.partial(prep_kernel, halves),
        "prep",
        [(half, BF)] * halves + [((2, 2, kv_count, rows, size), BF), ((2, 2, kv_count, rows, 128), F32)],
        (*(hbm(one) for one in own), *(flip(one) for one in own), near),
        specs=[HBM] * 4 + [VMEM] * 5,
        scratch=[pltpu.VMEM(queries.shape, BF)] * 3
        + [pltpu.VMEM(log_sums.shape, F32)]
        + [pltpu.SemaphoreType.DMA((1,)), pltpu.SemaphoreType.DMA((width // 32, 3))],
        mib=24,
    )
    far = [move(one, 4) for one in halves_near]

    def chunk(kv, distance, first, kind, name, after=()):
        return call(
            functools.partial(chunk_kernel, distance, first),
            name,
            [((2, kv.shape[0] // 2, rows, width), BF), (kv.shape, kind)],
            (docs, lay, sub, kv),
            scratch=[pltpu.VMEM(kv.shape, F32)],
            after=after,
        )

    ds_mid, sums = chunk(mid, 2, 0, BF, "mid")
    mid_back = move(sums, -2)
    ds_far, far_back = [None] * halves, [None] * halves
    token = (ds_mid,)
    for index in reversed(range(halves)):
        ds_far[index], sums = chunk(far[index], 4, index * each, BF, "far" + str(index), token)
        token = (ds_far[index],)
        far_back[index] = move(sums, -4)
    parts = (1, 1, halves)
    rest = (ds_mid, *ds_far, mid, *far)
    ds_near, near_sums, part = call(
        functools.partial(near_kernel, parts),
        "near",
        [((2, kv_count, rows, width), BF), (full, F32), (queries.shape, BF)],
        (docs, lay, sub, near, *rest),
        scratch=[pltpu.VMEM(full, F32)],
    )
    rest = (ds_near, *rest[: 1 + halves], near, *rest[1 + halves :])
    (mine,) = call(functools.partial(query_kernel, 0, parts), "query_own", [(queries.shape, F32)], rest)
    far_sums = [one[:each] for one in far_back] + [one[each:] for one in far_back]
    sums = near_sums + mid_back.astype(F32) + jnp.concatenate(far_sums, axis=0).astype(F32)
    query_grad, key_grad, val_grad = call(
        sum_kernel,
        "sums",
        [(queries.shape, BF)] + [(keys.shape, BF)] * 2,
        (mine, flip(part), sums),
    )
    return query_grad, key_grad, val_grad


def solution(mesh):
    rows = P(("dp", "seq"), None, None)
    return jax.shard_map(
        on_device,
        mesh=mesh,
        in_specs=(rows,) * 5 + (P(None, ("dp", "seq")), P("dp")),
        out_specs=(rows,) * 3,
        check_vma=False,
    )
```

time: 82.1 us -> 45.4 us (0.55)
  starting transfers between devices: 37 us -> 15.8 us
  matrix products: 15.9 us -> 0 us
  Pallas kernels: 0 us -> 15 us
  waiting for transfers between devices: 19.6 us -> 13.4 us
  local copies, waits for them, and re-layouts: 5.2 us -> 0.03 us
  other arithmetic: 2.62 us -> 0.1 us
    ppermute x16 -> x11, starting transfers between devices: 37 us -> 15.8 us  [the longest x6 14.6 us: move(): lax.ppermute(value, 'seq', [(i, i + steps) for i in range(count) if 0 <=...]
    dot_general x25 -> x0, matrix products: 15.9 us -> none  [the longest x5 3.92 us: gradients(): jnp.einsum('tkgd,skd->kgts', query_grp, key_blk, preferred_element_type=j...]
    pallas_call x0 -> x8, Pallas kernels: none -> 15 us  [call(): pl.pallas_call(run, in_specs=(specs or [VMEM] * count) + [VMEM] * len(aft...]
    ppermute x16 -> x11, waiting for transfers between devices: 19.6 us -> 13.4 us  [the longest x6 13.4 us: move(): lax.ppermute(value, 'seq', [(i, i + steps) for i in range(count) if 0 <=...]
    unnamed x17 -> x2, local copies, waits for them, and re-layouts: 5.14 us -> 0.01 us
    reduce_sum x1 -> x0, other arithmetic: 2.16 us -> none  [on_device(): jnp.sum(out_grad.astype(jnp.float32) * attn_out.astype(jnp.float32), axis...]
  transfers between devices with their start and end apart: 16 -> 11, of which waited for: 6 -> 3; matrix products, arithmetic and copies ran while one was open for 26% -> 0% of each run, Pallas kernels for 0% -> 30%
where the time goes in v2:
time: 45.4 us; the launch traced here: 45.1 us
  starting transfers between devices  15.8 us (35%)
  Pallas kernels  15 us (33%)
  waiting for transfers between devices  13.4 us (30%)
  between operations  0.83 us (2%)
    pallas_call x8, Pallas kernels, call(): pl.pallas_call(run, in_specs=(specs or [VMEM] * count) + [VMEM] * len(aft...  15 us
    ppermute x6, starting transfers between devices, move(): lax.ppermute(value, 'seq', [(i, i + steps) for i in range(count) if 0 <=...  14.6 us
    ppermute x6, waiting for transfers between devices, move(): lax.ppermute(value, 'seq', [(i, i + steps) for i in range(count) if 0 <=...  13.4 us
    ppermute x5, starting transfers between devices, flip(): return lax.ppermute(value, 'seq', [(i, i ^ 1) for i in range(count)])  1.18 us
  transfers between devices with their start and end apart: 11, of which 3 were waited for; matrix products, arithmetic and copies ran while one was open for 0% of the time, Pallas kernels for 30%

profile of v2, /device:TPU:0, one launch (start us, length us, event | category | flops | bytes accessed | tf_op | source)
XLA Modules:
  0.0 45.1 jit_solution(1945829698093134865)
XLA Ops:
  0.6 0.5 %collective-permute-start = (bf16[128,32,128]{2,1,0:T(8,128)(2,1)}, bf16[128,32,128]{2,1,0:T(8,128)(2,1)S(1)}, u32[]{:S(2)}, u32[]{:S(2)}) collective-permute-start(bf16[128,32,128]{2,1,0:T(8,128)(2,1)} %refs_0_.3), channel_id=1, source_target_pairs={{0,1},{1,0},{2,3},{3,2},{4,5},{5,4},{6,7},{7,6},{8,9},{9,8},{10,11... | collective-permute-start | bytes 3145736 | tf_op jit(solution)/shard_map/ppermute | solution.py:214
  1.1 0.1 collective-permute-start.2
  1.2 0.4 collective-permute-start.1
  1.7 0.1 collective-permute-start.3
  1.7 1.5 %pack.1.refs_8_.refs_3_.refs_4_ = bf16[8,128,128]{2,1,0:T(8,128)(2,1)S(1)} custom-call(bf16[128,4,128]{2,1,0:T(4,128)(2,1)} %refs_0_.2, bf16[128,4,128]{2,1,0:T(4,128)(2,1)} %refs_1_.2), custom_call_target="tpu_custom_call" | custom-call | flops 10000000000 | bytes 10000000 | tf_op jit(solution)/shard_map/pack/pallas_call | solution.py:36
  3.3 0.0 copy-start
  3.3 4.9 %collective-permute-start.4 = (bf16[8,128,128]{2,1,0:T(8,128)(2,1)S(1)}, bf16[8,128,128]{2,1,0:T(8,128)(2,1)S(1)}, u32[]{:S(2)}, u32[]{:S(2)}) collective-permute-start(bf16[8,128,128]{2,1,0:T(8,128)(2,1)S(1)} %pack.1.refs_8_.refs_3_.refs_4_), channel_id=1, source_target_pairs={{0,2},{1,3},{2,4},{3,5},{4,6},{5,7},{8,10},{9,11},{10,12},{11,13},... | collective-permute-start | bytes 786440 | tf_op jit(solution)/shard_map/ppermute | solution.py:217
  8.2 0.0 collective-permute-done.3.refs_7_
  8.2 0.0 collective-permute-done.refs_4_
  8.2 0.0 collective-permute-done.2.refs_6_
  8.3 0.0 collective-permute-done.1.refs_5_
  8.3 3.5 %prep.1 = (bf16[4,128,128]{2,1,0:T(8,128)(2,1)S(1)}, bf16[4,128,128]{2,1,0:T(8,128)(2,1)S(1)}, bf16[2,2,4,1024,128]{4,3,2,1,0:T(8,128)(2,1)S(1)}, f32[2,2,4,1024,128]{4,3,2,1,0:T(8,128)S(1)}) custom-call(bf16[128,32,128]{2,1,0:T(8,128)(2,1)} %refs_0_.3, bf16[128,32,128]{2,1,0:T(8,128)(2,1)} %refs_1_.3, bf16[128,32,128]{2,1,0:T(8,128)(2,1)} %refs_2_.1, ...), custom_call_target="tpu_custom_call" | custom-call | flops 10000000000 | bytes 10000000 | tf_op jit(solution)/shard_map/prep/pallas_call | solution.py:36
  11.7 4.5 %collective-permute-start.5 = (bf16[4,128,128]{2,1,0:T(8,128)(2,1)S(1)}, bf16[4,128,128]{2,1,0:T(8,128)(2,1)S(1)}, u32[]{:S(2)}, u32[]{:S(2)}) collective-permute-start(bf16[4,128,128]{2,1,0:T(8,128)(2,1)S(1)} %get-tuple-element.19), channel_id=1, source_target_pairs={{0,4},{1,5},{2,6},{3,7},{8,12},{9,13},{10,14},{11,15},{16,20},{17,... | collective-permute-start | bytes 393224 | tf_op jit(solution)/shard_map/ppermute | solution.py:217
  16.2 1.3 %collective-permute-start.6 = (bf16[4,128,128]{2,1,0:T(8,128)(2,1)S(1)}, bf16[4,128,128]{2,1,0:T(8,128)(2,1)S(1)}, u32[]{:S(2)}, u32[]{:S(2)}) collective-permute-start(bf16[4,128,128]{2,1,0:T(8,128)(2,1)S(1)} %get-tuple-element.20), channel_id=1, source_target_pairs={{0,4},{1,5},{2,6},{3,7},{8,12},{9,13},{10,14},{11,15},{16,20},{17,... | collective-permute-start | bytes 393224 | tf_op jit(solution)/shard_map/ppermute | solution.py:217
  17.5 0.0 collective-permute-done.4.refs_3_.refs_7_.refs_5_
  17.5 0.0 copy-done
  17.6 0.9 %mid.1 = (bf16[2,4,1024,128]{3,2,1,0:T(8,128)(2,1)S(1)}, bf16[8,128,128]{2,1,0:T(8,128)(2,1)S(1)}) custom-call(s32[8,128]{1,0:T(8,128)S(1)} %bitcast.1, bf16[2,2,4,1024,128]{4,3,2,1,0:T(8,128)(2,1)S(1)} %get-tuple-element.16.refs_1_, f32[2,2,4,1024,128]{4,3,2,1,0:T(8,128)S(1)} %get-tuple-element.17.refs_2_, ...), custom_call_target="tpu_custom_call" | custom-call | flops 10000000000 | bytes 10000000 | tf_op jit(solution)/shard_map/mid/pallas_call | solution.py:36
  18.5 1.3 %collective-permute-start.8 = (bf16[8,128,128]{2,1,0:T(8,128)(2,1)S(1)}, bf16[8,128,128]{2,1,0:T(8,128)(2,1)S(1)}, u32[]{:S(2)}, u32[]{:S(2)}) collective-permute-start(bf16[8,128,128]{2,1,0:T(8,128)(2,1)S(1)} %get-tuple-element.26), channel_id=1, source_target_pairs={{2,0},{3,1},{4,2},{5,3},{6,4},{7,5},{10,8},{11,9},{12,10},{13,11},... | collective-permute-start | bytes 786440 | tf_op jit(solution)/shard_map/ppermute | solution.py:217
  19.8 2.1 %collective-permute-done.6.refs_3_.refs_9_.refs_7_ = bf16[4,128,128]{2,1,0:T(8,128)(2,1)S(1)} collective-permute-done((bf16[4,128,128]{2,1,0:T(8,128)(2,1)S(1)}, bf16[4,128,128]{2,1,0:T(8,128)(2,1)S(1)}, u32[]{:S(2)}, u32[]{:S(2)}) %collective-permute-start.6) | collective-permute-done | bytes 131104 | tf_op jit(solution)/shard_map/ppermute | solution.py:217
  21.9 0.8 %far1.1 = (bf16[2,2,1024,128]{3,2,1,0:T(8,128)(2,1)S(1)}, bf16[4,128,128]{2,1,0:T(8,128)(2,1)S(1)}) custom-call(s32[8,128]{1,0:T(8,128)S(1)} %bitcast.2, bf16[2,2,4,1024,128]{4,3,2,1,0:T(8,128)(2,1)S(1)} %get-tuple-element.16.refs_1_, f32[2,2,4,1024,128]{4,3,2,1,0:T(8,128)S(1)} %get-tuple-element.17.refs_2_, ...), custom_call_target="tpu_custom_call" | custom-call | flops 10000000000 | bytes 10000000 | tf_op jit(solution)/shard_map/far1/pallas_call | solution.py:36
  22.7 1.3 %collective-permute-start.10 = (bf16[4,128,128]{2,1,0:T(8,128)(2,1)S(1)}, bf16[4,128,128]{2,1,0:T(8,128)(2,1)S(1)}, u32[]{:S(2)}, u32[]{:S(2)}) collective-permute-start(bf16[4,128,128]{2,1,0:T(8,128)(2,1)S(1)} %get-tuple-element.28), channel_id=1, source_target_pairs={{4,0},{5,1},{6,2},{7,3},{12,8},{13,9},{14,10},{15,11},{20,16},{21,... | collective-permute-start | bytes 393224 | tf_op jit(solution)/shard_map/ppermute | solution.py:217
  24.0 0.0 collective-permute-done.5.refs_3_.refs_8_.refs_6_
  24.0 0.8 %far0.1 = (bf16[2,2,1024,128]{3,2,1,0:T(8,128)(2,1)S(1)}, bf16[4,128,128]{2,1,0:T(8,128)(2,1)S(1)}) custom-call(s32[8,128]{1,0:T(8,128)S(1)} %bitcast.3, bf16[2,2,4,1024,128]{4,3,2,1,0:T(8,128)(2,1)S(1)} %get-tuple-element.16.refs_1_, f32[2,2,4,1024,128]{4,3,2,1,0:T(8,128)S(1)} %get-tuple-element.17.refs_2_, ...), custom_call_target="tpu_custom_call" | custom-call | flops 10000000000 | bytes 10000000 | tf_op jit(solution)/shard_map/far0/pallas_call | solution.py:36
  24.8 1.3 %collective-permute-start.9 = (bf16[4,128,128]{2,1,0:T(8,128)(2,1)S(1)}, bf16[4,128,128]{2,1,0:T(8,128)(2,1)S(1)}, u32[]{:S(2)}, u32[]{:S(2)}) collective-permute-start(bf16[4,128,128]{2,1,0:T(8,128)(2,1)S(1)} %get-tuple-element.27), channel_id=1, source_target_pairs={{4,0},{5,1},{6,2},{7,3},{12,8},{13,9},{14,10},{15,11},{20,16},{21,... | collective-permute-start | bytes 393224 | tf_op jit(solution)/shard_map/ppermute | solution.py:217
  26.1 5.1 %near.1 = (bf16[2,4,1024,128]{3,2,1,0:T(8,128)(2,1)S(1)}, f32[8,128,128]{2,1,0:T(8,128)S(1)}, bf16[128,32,128]{2,1,0:T(8,128)(2,1)S(1)}) custom-call(s32[8,128]{1,0:T(8,128)S(1)} %bitcast.4, bf16[2,2,4,1024,128]{4,3,2,1,0:T(8,128)(2,1)S(1)} %get-tuple-element.16.refs_1_, f32[2,2,4,1024,128]{4,3,2,1,0:T(8,128)S(1)} %get-tuple-element.17.refs_2_, ...), custom_call_target="tpu_custom_call" | custom-call | flops 10000000000 | bytes 10000000 | tf_op jit(solution)/shard_map/near/pallas_call | solution.py:36
  31.2 0.1 collective-permute-start.7
  31.3 1.0 %query_own.1.refs_0_ = f32[128,32,128]{2,1,0:T(8,128)S(1)} custom-call(bf16[2,4,1024,128]{3,2,1,0:T(8,128)(2,1)S(1)} %get-tuple-element.23.refs_0_, bf16[2,4,1024,128]{3,2,1,0:T(8,128)(2,1)S(1)} %get-tuple-element.18.refs_4_.refs_1_, bf16[2,2,1024,128]{3,2,1,0:T(8,128)(2,1)S(1)} %get-tuple-element.22.refs_5_.refs_2_, ...), custom_call_target="tpu_custom_call" | custom-call | flops 10000000000 | bytes 10000000 | tf_op jit(solution)/shard_map/query_own/pallas_call | solution.py:36
  32.3 9.6 %collective-permute-done.10 = bf16[4,128,128]{2,1,0:T(8,128)(2,1)S(1)} collective-permute-done((bf16[4,128,128]{2,1,0:T(8,128)(2,1)S(1)}, bf16[4,128,128]{2,1,0:T(8,128)(2,1)S(1)}, u32[]{:S(2)}, u32[]{:S(2)}) %collective-permute-start.10) | collective-permute-done | bytes 131104 | tf_op jit(solution)/shard_map/ppermute | solution.py:217
  41.8 1.7 %collective-permute-done.9 = bf16[4,128,128]{2,1,0:T(8,128)(2,1)S(1)} collective-permute-done((bf16[4,128,128]{2,1,0:T(8,128)(2,1)S(1)}, bf16[4,128,128]{2,1,0:T(8,128)(2,1)S(1)}, u32[]{:S(2)}, u32[]{:S(2)}) %collective-permute-start.9) | collective-permute-done | bytes 131104 | tf_op jit(solution)/shard_map/ppermute | solution.py:217
  43.5 0.0 collective-permute-done.8
  43.5 0.1 convert_add_fusion.refs_2_
  43.6 0.0 collective-permute-done.7.refs_1_
  43.6 1.4 %sums.1 = (bf16[128,32,128]{2,1,0:T(8,128)(2,1)}, bf16[128,4,128]{2,1,0:T(4,128)(2,1)}, bf16[128,4,128]{2,1,0:T(4,128)(2,1)}) custom-call(f32[128,32,128]{2,1,0:T(8,128)S(1)} %query_own.1.refs_0_, bf16[128,32,128]{2,1,0:T(8,128)(2,1)S(1)} %collective-permute-done.7.refs_1_, f32[8,128,128]{2,1,0:T(8,128)S(1)} %convert_add_fusion.refs_2_), custom_call_target="tpu_custom_call" | custom-call | flops 10000000000 | bytes 10000000 | tf_op jit(solution)/shard_map/sums/pallas_call | solution.py:36
  (2 shorter events, 0.0 us)
Async XLA Ops:
  0.6 7.6 %collective-permute-start = (bf16[128,32,128]{2,1,0:T(8,128)(2,1)}, bf16[128,32,128]{2,1,0:T(8,128)(2,1)S(1)}, u32[]{:S(2)}, u32[]{:S(2)}) collective-permute-start(bf16[128,32,128]{2,1,0:T(8,128)(2,1)} %refs_0_.3), channel_id=1, source_target_pairs={{0,1},{1,0},{2,3},{3,2},{4,5},{5,4},{6,7},{7,6},{8,9},{9,8},{10,11... | collective-permute-start | bytes 3145736 | tf_op jit(solution)/shard_map/ppermute | solution.py:214
  1.1 7.1 %collective-permute-start.2 = (bf16[128,32,128]{2,1,0:T(8,128)(2,1)}, bf16[128,32,128]{2,1,0:T(8,128)(2,1)S(1)}, u32[]{:S(2)}, u32[]{:S(2)}) collective-permute-start(bf16[128,32,128]{2,1,0:T(8,128)(2,1)} %refs_2_.1), channel_id=1, source_target_pairs={{0,1},{1,0},{2,3},{3,2},{4,5},{5,4},{6,7},{7,6},{8,9},{9,8},{10,11... | collective-permute-start | bytes 3145736 | tf_op jit(solution)/shard_map/ppermute | solution.py:214
  1.2 7.0 %collective-permute-start.1 = (bf16[128,32,128]{2,1,0:T(8,128)(2,1)}, bf16[128,32,128]{2,1,0:T(8,128)(2,1)S(1)}, u32[]{:S(2)}, u32[]{:S(2)}) collective-permute-start(bf16[128,32,128]{2,1,0:T(8,128)(2,1)} %refs_1_.3), channel_id=1, source_target_pairs={{0,1},{1,0},{2,3},{3,2},{4,5},{5,4},{6,7},{7,6},{8,9},{9,8},{10,11... | collective-permute-start | bytes 3145736 | tf_op jit(solution)/shard_map/ppermute | solution.py:214
  1.7 6.6 %collective-permute-start.3 = (f32[32,128]{1,0:T(8,128)}, f32[32,128]{1,0:T(8,128)S(1)}, u32[]{:S(2)}, u32[]{:S(2)}) collective-permute-start(f32[32,128]{1,0:T(8,128)} %refs_3_.1), channel_id=1, source_target_pairs={{0,1},{1,0},{2,3},{3,2},{4,5},{5,4},{6,7},{7,6},{8,9},{9,8},{10,11... | collective-permute-start | bytes 49160 | tf_op jit(solution)/shard_map/ppermute | solution.py:214
  3.3 14.3 %copy-start = (s32[1024]{0:T(1024)S(1)}, s32[1024]{0:T(1024)}, u32[]{:S(2)}) copy-start(s32[1024]{0:T(1024)} %param.13) | copy-start | bytes 12292
  3.3 14.2 %collective-permute-start.4 = (bf16[8,128,128]{2,1,0:T(8,128)(2,1)S(1)}, bf16[8,128,128]{2,1,0:T(8,128)(2,1)S(1)}, u32[]{:S(2)}, u32[]{:S(2)}) collective-permute-start(bf16[8,128,128]{2,1,0:T(8,128)(2,1)S(1)} %pack.1.refs_8_.refs_3_.refs_4_), channel_id=1, source_target_pairs={{0,2},{1,3},{2,4},{3,5},{4,6},{5,7},{8,10},{9,11},{10,12},{11,13},... | collective-permute-start | bytes 786440 | tf_op jit(solution)/shard_map/ppermute | solution.py:217
  11.7 12.2 %collective-permute-start.5 = (bf16[4,128,128]{2,1,0:T(8,128)(2,1)S(1)}, bf16[4,128,128]{2,1,0:T(8,128)(2,1)S(1)}, u32[]{:S(2)}, u32[]{:S(2)}) collective-permute-start(bf16[4,128,128]{2,1,0:T(8,128)(2,1)S(1)} %get-tuple-element.19), channel_id=1, source_target_pairs={{0,4},{1,5},{2,6},{3,7},{8,12},{9,13},{10,14},{11,15},{16,20},{17,... | collective-permute-start | bytes 393224 | tf_op jit(solution)/shard_map/ppermute | solution.py:217
  16.2 5.7 %collective-permute-start.6 = (bf16[4,128,128]{2,1,0:T(8,128)(2,1)S(1)}, bf16[4,128,128]{2,1,0:T(8,128)(2,1)S(1)}, u32[]{:S(2)}, u32[]{:S(2)}) collective-permute-start(bf16[4,128,128]{2,1,0:T(8,128)(2,1)S(1)} %get-tuple-element.20), channel_id=1, source_target_pairs={{0,4},{1,5},{2,6},{3,7},{8,12},{9,13},{10,14},{11,15},{16,20},{17,... | collective-permute-start | bytes 393224 | tf_op jit(solution)/shard_map/ppermute | solution.py:217
  18.5 25.0 %collective-permute-start.8 = (bf16[8,128,128]{2,1,0:T(8,128)(2,1)S(1)}, bf16[8,128,128]{2,1,0:T(8,128)(2,1)S(1)}, u32[]{:S(2)}, u32[]{:S(2)}) collective-permute-start(bf16[8,128,128]{2,1,0:T(8,128)(2,1)S(1)} %get-tuple-element.26), channel_id=1, source_target_pairs={{2,0},{3,1},{4,2},{5,3},{6,4},{7,5},{10,8},{11,9},{12,10},{13,11},... | collective-permute-start | bytes 786440 | tf_op jit(solution)/shard_map/ppermute | solution.py:217
  22.7 19.1 %collective-permute-start.10 = (bf16[4,128,128]{2,1,0:T(8,128)(2,1)S(1)}, bf16[4,128,128]{2,1,0:T(8,128)(2,1)S(1)}, u32[]{:S(2)}, u32[]{:S(2)}) collective-permute-start(bf16[4,128,128]{2,1,0:T(8,128)(2,1)S(1)} %get-tuple-element.28), channel_id=1, source_target_pairs={{4,0},{5,1},{6,2},{7,3},{12,8},{13,9},{14,10},{15,11},{20,16},{21,... | collective-permute-start | bytes 393224 | tf_op jit(solution)/shard_map/ppermute | solution.py:217
  24.8 18.7 %collective-permute-start.9 = (bf16[4,128,128]{2,1,0:T(8,128)(2,1)S(1)}, bf16[4,128,128]{2,1,0:T(8,128)(2,1)S(1)}, u32[]{:S(2)}, u32[]{:S(2)}) collective-permute-start(bf16[4,128,128]{2,1,0:T(8,128)(2,1)S(1)} %get-tuple-element.27), channel_id=1, source_target_pairs={{4,0},{5,1},{6,2},{7,3},{12,8},{13,9},{14,10},{15,11},{20,16},{21,... | collective-permute-start | bytes 393224 | tf_op jit(solution)/shard_map/ppermute | solution.py:217
  31.2 12.4 %collective-permute-start.7 = (bf16[128,32,128]{2,1,0:T(8,128)(2,1)S(1)}, bf16[128,32,128]{2,1,0:T(8,128)(2,1)S(1)}, u32[]{:S(2)}, u32[]{:S(2)}) collective-permute-start(bf16[128,32,128]{2,1,0:T(8,128)(2,1)S(1)} %get-tuple-element.24), channel_id=1, source_target_pairs={{0,1},{1,0},{2,3},{3,2},{4,5},{5,4},{6,7},{7,6},{8,9},{9,8},{10,11... | collective-permute-start | bytes 3145736 | tf_op jit(solution)/shard_map/ppermute | solution.py:214

commit v3 on v2

v3 whole, which is shorter than its diff:
```python
import functools

import jax
import jax.numpy as jnp
from jax import lax
from jax.experimental import pallas as pl
from jax.experimental.pallas import tpu as pltpu
from jax.sharding import PartitionSpec as P

COSTS = {
    "pack": 10,
    "prep_early": 10,
    "prep_late": 10,
    "near_early": 10,
    "mid": 10,
    "far": 10,
    "near": 10,
    "query_own": 10,
    "sums": 10,
}
EARLY_HEADS = 4
LOG2E = 1.4426950408889634
HBM = pl.BlockSpec(memory_space=pltpu.HBM)
VMEM = pl.BlockSpec(memory_space=pltpu.VMEM)
NT = (((1,), (1,)), ((), ()))
TN = (((0,), (0,)), ((), ()))
BF = jnp.bfloat16
F32 = jnp.float32


def call(kernel, name, shapes, operands, specs=None, scratch=(), after=(), mib=8, aliases=None):
    count = len(operands)

    def run(*refs):
        kernel(*refs[:count], *refs[count + len(after) :])

    return pl.pallas_call(
        run,
        in_specs=(specs or [VMEM] * count) + [VMEM] * len(after),
        out_specs=[VMEM] * len(shapes),
        out_shape=[jax.ShapeDtypeStruct(*one) for one in shapes],
        scratch_shapes=scratch,
        compiler_params=pltpu.CompilerParams(vmem_limit_bytes=mib * 1024 * 1024),
        cost_estimate=pl.CostEstimate(flops=int(COSTS[name] * 1e9), bytes_accessed=10**7, transcendentals=0),
        input_output_aliases=aliases or {},
        name=name,
    )(*operands, *after)


def split3(value):
    high = value.astype(BF).astype(F32)
    rest = value - high
    middle = rest.astype(BF).astype(F32)
    return high, middle, rest - middle


def start_copies(pairs, sems):
    copies = []
    for i, (source, target) in enumerate(pairs):
        copies.append(pltpu.make_async_copy(source, target, sems.at[i]))
        copies[-1].start()
    return copies


def pack_kernel(k_hbm, v_hbm, all_ref, k_ref, v_ref, sems):
    copies = start_copies(((k_hbm, k_ref), (v_hbm, v_ref)), sems)
    kv_count = k_ref.shape[1]
    for i, ref in enumerate((k_ref, v_ref)):
        copies[i].wait()
        for kv in range(kv_count):
            all_ref[i * kv_count + kv] = ref[:, kv, :]


def prep_kernel(q_hbm, g_hbm, o_hbm, log_hbm, q1_ref, g1_ref, o1_ref, log1_ref, *refs):
    rows_ref, sub_ref, q_ref, g_ref, o_ref, log_ref, log_sem, sems = refs
    rows, heads, size = q_ref.shape
    kv_count = rows_ref.shape[2]
    group = heads // kv_count
    step = 32
    log_copy = start_copies(((log_hbm, log_ref),), log_sem)[0]
    copies = []
    for i, at in enumerate(range(0, rows, step)):
        part = pl.ds(at, step)
        pairs = [(one.at[part], two.at[part]) for one, two in ((g_hbm, g_ref), (o_hbm, o_ref), (q_hbm, q_ref))]
        copies.append(start_copies(pairs, sems.at[i]))
    lane_row = lax.broadcasted_iota(jnp.int32, (rows, 128), 1)
    lane = lax.broadcasted_iota(jnp.int32, (1, heads, 128), 2)
    head = lax.broadcasted_iota(jnp.int32, (1, heads, 128), 1)
    own = (lane == head) | (lane == head + heads) | (lane == head + 2 * heads)
    ones = jnp.where(lax.broadcasted_iota(jnp.int32, (128, 128), 0) < 3 * heads, 1.0, 0.0).astype(BF)
    for side, (q_one, g_one, o_one, log_one) in (
        (1, (q1_ref, g1_ref, o1_ref, log1_ref)),
        (0, (q_ref, g_ref, o_ref, log_ref)),
    ):
        if side == 0:
            log_copy.wait()
        logs = jnp.concatenate([log_one[...] * LOG2E] * (128 // heads), axis=0).T
        l_high, l_mid, l_low = split3(logs)
        logs = jnp.where(lane_row < heads, l_high, jnp.where(lane_row < 2 * heads, l_mid, l_low))
        for i, at in enumerate(range(0, rows, step)):
            part = slice(at, at + step)
            if side == 0:
                for one in copies[i]:
                    one.wait()
            grad, query = g_one[part], q_one[part]
            delta = jnp.sum(grad.astype(F32) * o_one[part].astype(F32), axis=-1, keepdims=True)
            delta = jnp.broadcast_to(delta, (step, heads, 128))
            aux = jnp.where(own, logs[part, None, :], 0.0).astype(BF)
            spot = slice(at * group, (at + step) * group)
            for kv in range(kv_count):
                span = slice(kv * group, (kv + 1) * group)
                rows_ref[side, 0, kv, spot] = query[:, span, :].reshape(step * group, size)
                rows_ref[side, 1, kv, spot] = grad[:, span, :].reshape(step * group, size)
                sub_ref[side, 0, kv, spot] = jnp.dot(
                    aux[:, span, :].reshape(step * group, 128), ones, preferred_element_type=F32
                )
                sub_ref[side, 1, kv, spot] = delta[:, span, :].reshape(step * group, 128)


def sends_far():
    return lax.axis_index("seq") + 4 < lax.axis_size("seq")


def prep_early_kernel(*refs):
    @pl.when(sends_far())
    def _():
        prep_kernel(*refs)


def prep_late_kernel(*refs):
    @pl.when(jnp.logical_not(sends_far()))
    def _():
        prep_kernel(*refs[:8], *refs[10:])


def chunk_kernel(distance, doc_ref, rows_ref, sub_ref, kv_ref, ds_ref, out_ref, acc, early=None):
    count, size = rows_ref.shape[3:]
    each, width = kv_ref.shape[0] // 2, kv_ref.shape[1]
    rows = width
    scale = size ** (-0.5)
    shard = lax.axis_index("seq")
    key_shard = shard - distance
    key_doc = doc_ref[pl.ds(jnp.maximum(key_shard, 0), 1), :]
    if early is None:
        acc[...] = jnp.zeros_like(acc)
    for side in range(2):
        query_shard = shard ^ side
        query_rows = jnp.broadcast_to(doc_ref[pl.ds(query_shard, 1), :], (rows, rows)).T
        ends = jnp.sum((query_rows <= key_doc).astype(jnp.int32), axis=0, keepdims=True)
        live = (key_shard >= 0) & (key_shard <= query_shard) & (jnp.max(ends) > 0)

        def heads(these):
            pos = lax.broadcasted_iota(jnp.int32, (rows, count // rows, width), 0).reshape(count, width)
            low = (key_shard - query_shard) * width + lax.broadcasted_iota(jnp.int32, (1, width), 1)
            mask = (pos >= low) & (pos < ends)
            for j in these:
                query, grad = rows_ref[side, 0, j], rows_ref[side, 1, j]
                logits = lax.dot_general(query, kv_ref[j], NT, preferred_element_type=F32)
                logits = logits * (scale * LOG2E) - sub_ref[side, 0, j]
                probs = jnp.where(mask, jnp.exp2(logits), 0.0)
                diff = lax.dot_general(grad, kv_ref[each + j], NT, preferred_element_type=F32)
                ds = (probs * (diff - sub_ref[side, 1, j])).astype(BF)
                ds_ref[side, j] = ds
                sums = lax.dot_general(
                    jnp.concatenate([ds, probs.astype(BF)], axis=1),
                    jnp.concatenate([query, grad], axis=1),
                    TN,
                    preferred_element_type=F32,
                )
                acc[j] += sums[:width, :size] * scale
                acc[each + j] += sums[width:, size:]

        if early == "only":
            if side == 0:
                heads(range(EARLY_HEADS))
            continue
        if early == "rest" and side == 0:
            pl.when(jnp.logical_not(sends_far()))(functools.partial(heads, range(EARLY_HEADS)))
            heads(range(EARLY_HEADS, each))
            continue
        pl.when(live)(functools.partial(heads, range(each)))

        @pl.when(jnp.logical_not(live))
        def _():
            ds_ref[side] = jnp.zeros(ds_ref.shape[1:], BF)

    out_ref[...] = acc[...].astype(out_ref.dtype)


def query_kernel(side, ds0_ref, ds1_ref, ds2_ref, kv0_ref, kv1_ref, kv2_ref, out_ref):
    rows, heads, size = out_ref.shape
    kv_count = kv0_ref.shape[0] // 2
    group = heads // kv_count
    for kv in range(kv_count):
        ds = jnp.concatenate([one[side, kv] for one in (ds0_ref, ds1_ref, ds2_ref)], axis=1)
        key = jnp.concatenate([one[kv] for one in (kv0_ref, kv1_ref, kv2_ref)], axis=0)
        got = jnp.dot(ds, key, preferred_element_type=F32) * size ** (-0.5)
        out_ref[:, kv * group : (kv + 1) * group, :] = got.reshape(rows, group, size).astype(out_ref.dtype)


def near_early_kernel(doc_ref, rows_ref, sub_ref, kv_ref, copy_ref, ds_ref, acc):
    copy_ref[...] = kv_ref[...]

    @pl.when(sends_far())
    def _():
        acc[...] = jnp.zeros_like(acc)
        chunk_kernel(0, doc_ref, rows_ref, sub_ref, kv_ref, ds_ref, acc, acc, "only")


def near_kernel(
    doc_ref, rows_ref, sub_ref, kv_ref, _, sums_in, ds1_ref, ds2_ref, kv1_ref, kv2_ref, ds_ref, out_ref, query_ref, acc
):
    acc[...] = jnp.zeros_like(acc)

    @pl.when(sends_far())
    def _():
        acc[...] = sums_in[...]

    chunk_kernel(0, doc_ref, rows_ref, sub_ref, kv_ref, ds_ref, out_ref, acc, "rest")
    query_kernel(1, ds_ref, ds1_ref, ds2_ref, kv_ref, kv1_ref, kv2_ref, query_ref)


def sum_kernel(one_ref, two_ref, sums_ref, query_ref, key_ref, val_ref):
    query_ref[...] = (one_ref[...] + two_ref[...].astype(F32)).astype(BF)
    kv_count = key_ref.shape[1]
    for i, ref in enumerate((key_ref, val_ref)):
        heads = [sums_ref[i * kv_count + kv] for kv in range(kv_count)]
        ref[...] = jnp.stack(heads, axis=1).astype(BF)


def on_device(queries, keys, values, attn_out, out_grad, log_sums, doc_ids):
    width, heads, size = queries.shape
    kv_count = keys.shape[1]
    count = lax.axis_size("seq")
    docs = doc_ids.reshape(-1, width)
    rows = width * heads // kv_count
    full = (2 * kv_count, width, size)

    def flip(value):
        return lax.ppermute(value, "seq", [(i, i ^ 1) for i in range(count)])

    def move(value, steps, parity=None):
        pairs = [(i, i + steps) for i in range(count) if 0 <= i + steps < count]
        return lax.ppermute(value, "seq", [one for one in pairs if parity in (None, one[0] // 2 % 2)])

    hbm = functools.partial(pltpu.with_memory_space_constraint, memory_space=pltpu.HBM)
    (near,) = call(
        pack_kernel,
        "pack",
        [(full, BF)],
        (hbm(keys), hbm(values)),
        specs=[HBM] * 2,
        scratch=[pltpu.VMEM(keys.shape, BF)] * 2 + [pltpu.SemaphoreType.DMA((2,))],
    )
    mid = move(near, 2)
    own = (queries, out_grad, attn_out, log_sums)
    own = tuple(hbm(one) for one in own) + tuple(flip(one) for one in own)
    laid = [((2, 2, kv_count, rows, size), BF), ((2, 2, kv_count, rows, 128), F32)]
    prep = dict(
        specs=[HBM] * 4 + [VMEM] * 4,
        scratch=[pltpu.VMEM(queries.shape, BF)] * 3
        + [pltpu.VMEM(log_sums.shape, F32)]
        + [pltpu.SemaphoreType.DMA((1,)), pltpu.SemaphoreType.DMA((width // 32, 3))],
        mib=24,
    )
    lay, sub = call(prep_early_kernel, "prep_early", laid, own, **prep)
    copied, ds_near, near_sums = call(
        near_early_kernel,
        "near_early",
        [(full, BF), ((2, kv_count, rows, width), BF), (full, F32)],
        (docs, lay, sub, near),
    )
    far = move(copied, 4)
    prep["specs"] = [HBM] * 4 + [VMEM] * 6
    lay, sub = call(prep_late_kernel, "prep_late", laid, (*own, lay, sub), aliases={8: 0, 9: 1}, **prep)

    def chunk(kv, distance, name, after=()):
        return call(
            functools.partial(chunk_kernel, distance),
            name,
            [((2, kv_count, rows, width), BF), (full, BF)],
            (docs, lay, sub, kv),
            scratch=[pltpu.VMEM(full, F32)],
            after=after,
        )

    ds_mid, mid_sums = chunk(mid, 2, "mid")
    mid_back = move(mid_sums, -2)
    ds_far, far_sums = chunk(far, 4, "far", (ds_mid,))
    far_back = move(far_sums, -4)
    ds_near, near_sums, part = call(
        near_kernel,
        "near",
        [((2, kv_count, rows, width), BF), (full, F32), (queries.shape, BF)],
        (docs, lay, sub, near, ds_near, near_sums, ds_mid, ds_far, mid, far),
        scratch=[pltpu.VMEM(full, F32)],
        aliases={4: 0},
    )
    (mine,) = call(
        functools.partial(query_kernel, 0),
        "query_own",
        [(queries.shape, F32)],
        (ds_near, ds_mid, ds_far, near, mid, far),
    )
    sums = near_sums + mid_back.astype(F32) + far_back.astype(F32)
    query_grad, key_grad, val_grad = call(
        sum_kernel,
        "sums",
        [(queries.shape, BF)] + [(keys.shape, BF)] * 2,
        (mine, flip(part), sums),
    )
    return query_grad, key_grad, val_grad


def solution(mesh):
    rows = P(("dp", "seq"), None, None)
    return jax.shard_map(
        on_device,
        mesh=mesh,
        in_specs=(rows,) * 5 + (P(None, ("dp", "seq")), P("dp")),
        out_specs=(rows,) * 3,
        check_vma=False,
    )
```

time: 45.4 us -> 41.6 us (0.916); the launches traced: 45.1 us -> 42 us
  starting transfers between devices: 15.8 us -> 9.99 us
  waiting for transfers between devices: 13.4 us -> 17.4 us
  Pallas kernels: 15 us -> 13.8 us
    ppermute x6 -> x4, starting transfers between devices: 14.6 us -> 8.81 us  [move(): lax.ppermute(value, 'seq', [one for one in pairs if parity in (None, one[...]
    ppermute x6 -> x4, waiting for transfers between devices: 13.4 us -> 17.3 us  [move(): lax.ppermute(value, 'seq', [one for one in pairs if parity in (None, one[...]
    pallas_call x8 -> x9, Pallas kernels: 15 us -> 13.8 us  [call(): pl.pallas_call(run, in_specs=(specs or [VMEM] * count) + [VMEM] * len(aft...]
  transfers between devices with their start and end apart: 11 -> 9, of which waited for: 3 -> 3; matrix products, arithmetic and copies ran while one was open for 0% -> 0% of each run, Pallas kernels for 30% -> 29%
where the time goes in v3:
time: 41.6 us; the launch traced here: 42 us
  waiting for transfers between devices  17.4 us (42%)
  Pallas kernels  13.8 us (33%)
  starting transfers between devices  9.99 us (24%)
  between operations  0.8 us (2%)
    ppermute x4, waiting for transfers between devices, move(): lax.ppermute(value, 'seq', [one for one in pairs if parity in (None, one[...  17.3 us
    pallas_call x9, Pallas kernels, call(): pl.pallas_call(run, in_specs=(specs or [VMEM] * count) + [VMEM] * len(aft...  13.8 us
    ppermute x4, starting transfers between devices, move(): lax.ppermute(value, 'seq', [one for one in pairs if parity in (None, one[...  8.81 us
    ppermute x5, starting transfers between devices, flip(): return lax.ppermute(value, 'seq', [(i, i ^ 1) for i in range(count)])  1.18 us
  transfers between devices with their start and end apart: 9, of which 3 were waited for; matrix products, arithmetic and copies ran while one was open for 0% of the time, Pallas kernels for 29%

profile of v3, /device:TPU:0, one launch (start us, length us, event | category | flops | bytes accessed | tf_op | source)
XLA Modules:
  0.0 42.0 jit_solution(11321947033058476756)
XLA Ops:
  0.6 0.5 %collective-permute-start = (bf16[128,32,128]{2,1,0:T(8,128)(2,1)}, bf16[128,32,128]{2,1,0:T(8,128)(2,1)S(1)}, u32[]{:S(2)}, u32[]{:S(2)}) collective-permute-start(bf16[128,32,128]{2,1,0:T(8,128)(2,1)} %refs_0_.4), channel_id=1, source_target_pairs={{0,1},{1,0},{2,3},{3,2},{4,5},{5,4},{6,7},{7,6},{8,9},{9,8},{10,11... | collective-permute-start | bytes 3145736 | tf_op jit(solution)/shard_map/ppermute | solution.py:240
  1.1 0.1 collective-permute-start.1
  1.2 0.4 %collective-permute-start.2 = (bf16[128,32,128]{2,1,0:T(8,128)(2,1)}, bf16[128,32,128]{2,1,0:T(8,128)(2,1)S(1)}, u32[]{:S(2)}, u32[]{:S(2)}) collective-permute-start(bf16[128,32,128]{2,1,0:T(8,128)(2,1)} %refs_2_.3), channel_id=1, source_target_pairs={{0,1},{1,0},{2,3},{3,2},{4,5},{5,4},{6,7},{7,6},{8,9},{9,8},{10,11... | collective-permute-start | bytes 3145736 | tf_op jit(solution)/shard_map/ppermute | solution.py:240
  1.7 0.1 collective-permute-start.3
  1.7 1.5 %pack.1.refs_3_ = bf16[8,128,128]{2,1,0:T(8,128)(2,1)S(1)} custom-call(bf16[128,4,128]{2,1,0:T(4,128)(2,1)} %refs_0_.5, bf16[128,4,128]{2,1,0:T(4,128)(2,1)} %refs_1_.5), custom_call_target="tpu_custom_call" | custom-call | flops 10000000000 | bytes 10000000 | tf_op jit(solution)/shard_map/pack/pallas_call | solution.py:37
  3.3 0.0 copy-start
  3.3 4.9 %collective-permute-start.4 = (bf16[8,128,128]{2,1,0:T(8,128)(2,1)S(1)}, bf16[8,128,128]{2,1,0:T(8,128)(2,1)S(1)}, u32[]{:S(2)}, u32[]{:S(2)}) collective-permute-start(bf16[8,128,128]{2,1,0:T(8,128)(2,1)S(1)} %pack.1.refs_3_), channel_id=1, source_target_pairs={{0,2},{1,3},{2,4},{3,5},{4,6},{5,7},{8,10},{9,11},{10,12},{11,13},... | collective-permute-start | bytes 786440 | tf_op jit(solution)/shard_map/ppermute | solution.py:244
  8.2 0.0 collective-permute-done.3.refs_7_
  8.2 0.0 collective-permute-done.refs_4_
  8.2 0.0 collective-permute-done.1.refs_5_
  8.3 0.0 collective-permute-done.2.refs_6_
  8.3 2.8 %prep_early.1 = (bf16[2,2,4,1024,128]{4,3,2,1,0:T(8,128)(2,1)S(1)}, f32[2,2,4,1024,128]{4,3,2,1,0:T(8,128)S(1)}) custom-call(bf16[128,32,128]{2,1,0:T(8,128)(2,1)} %refs_0_.4, bf16[128,32,128]{2,1,0:T(8,128)(2,1)} %refs_1_.4, bf16[128,32,128]{2,1,0:T(8,128)(2,1)} %refs_2_.3, f32[32,128]{1,0:T(8,128)} %refs_3_.3, ...), custom_call_target="tpu_custom_call" | custom-call | flops 10000000000 | bytes 10000000 | tf_op jit(solution)/shard_map/prep_early/pallas_call | solution.py:37
  11.1 0.0 copy-done
  11.1 1.7 %near_early.1 = (bf16[8,128,128]{2,1,0:T(8,128)(2,1)S(1)}, bf16[2,4,1024,128]{3,2,1,0:T(8,128)(2,1)S(1)}, f32[8,128,128]{2,1,0:T(8,128)S(1)}) custom-call(s32[8,128]{1,0:T(8,128)S(1)} %bitcast.1, bf16[2,2,4,1024,128]{4,3,2,1,0:T(8,128)(2,1)S(1)} %get-tuple-element.17.refs_8_.refs_1_, f32[2,2,4,1024,128]{4,3,2,1,0:T(8,128)S(1)} %get-tuple-element.18.refs_9_.refs_2_, ...), custom_call_target="tpu_custom_call" | custom-call | flops 10000000000 | bytes 10000000 | tf_op jit(solution)/shard_map/near_early/pallas_call | solution.py:37
  12.8 1.3 %collective-permute-start.5 = (bf16[8,128,128]{2,1,0:T(8,128)(2,1)S(1)}, bf16[8,128,128]{2,1,0:T(8,128)(2,1)S(1)}, u32[]{:S(2)}, u32[]{:S(2)}) collective-permute-start(bf16[8,128,128]{2,1,0:T(8,128)(2,1)S(1)} %get-tuple-element.24), channel_id=1, source_target_pairs={{0,4},{1,5},{2,6},{3,7},{8,12},{9,13},{10,14},{11,15},{16,20},{17,... | collective-permute-start | bytes 786440 | tf_op jit(solution)/shard_map/ppermute | solution.py:244
  14.1 0.1 prep_late.1
  14.3 0.0 collective-permute-done.4.refs_3_.refs_8_.refs_4_
  14.3 0.9 %mid.1 = (bf16[2,4,1024,128]{3,2,1,0:T(8,128)(2,1)S(1)}, bf16[8,128,128]{2,1,0:T(8,128)(2,1)S(1)}) custom-call(s32[8,128]{1,0:T(8,128)S(1)} %bitcast.2, bf16[2,2,4,1024,128]{4,3,2,1,0:T(8,128)(2,1)S(1)} %get-tuple-element.19.refs_1_, f32[2,2,4,1024,128]{4,3,2,1,0:T(8,128)S(1)} %get-tuple-element.20.refs_2_, ...), custom_call_target="tpu_custom_call" | custom-call | flops 10000000000 | bytes 10000000 | tf_op jit(solution)/shard_map/mid/pallas_call | solution.py:37
  15.2 1.3 %collective-permute-start.7 = (bf16[8,128,128]{2,1,0:T(8,128)(2,1)S(1)}, bf16[8,128,128]{2,1,0:T(8,128)(2,1)S(1)}, u32[]{:S(2)}, u32[]{:S(2)}) collective-permute-start(bf16[8,128,128]{2,1,0:T(8,128)(2,1)S(1)} %get-tuple-element.29), channel_id=1, source_target_pairs={{2,0},{3,1},{4,2},{5,3},{6,4},{7,5},{10,8},{11,9},{12,10},{13,11},... | collective-permute-start | bytes 786440 | tf_op jit(solution)/shard_map/ppermute | solution.py:244
  16.5 3.4 %collective-permute-done.5.refs_3_.refs_9_.refs_5_ = bf16[8,128,128]{2,1,0:T(8,128)(2,1)S(1)} collective-permute-done((bf16[8,128,128]{2,1,0:T(8,128)(2,1)S(1)}, bf16[8,128,128]{2,1,0:T(8,128)(2,1)S(1)}, u32[]{:S(2)}, u32[]{:S(2)}) %collective-permute-start.5) | collective-permute-done | bytes 262176 | tf_op jit(solution)/shard_map/ppermute | solution.py:244
  19.9 1.1 %far.1 = (bf16[2,4,1024,128]{3,2,1,0:T(8,128)(2,1)S(1)}, bf16[8,128,128]{2,1,0:T(8,128)(2,1)S(1)}) custom-call(s32[8,128]{1,0:T(8,128)S(1)} %bitcast.3, bf16[2,2,4,1024,128]{4,3,2,1,0:T(8,128)(2,1)S(1)} %get-tuple-element.19.refs_1_, f32[2,2,4,1024,128]{4,3,2,1,0:T(8,128)S(1)} %get-tuple-element.20.refs_2_, ...), custom_call_target="tpu_custom_call" | custom-call | flops 10000000000 | bytes 10000000 | tf_op jit(solution)/shard_map/far/pallas_call | solution.py:37
  21.0 1.3 %collective-permute-start.8 = (bf16[8,128,128]{2,1,0:T(8,128)(2,1)S(1)}, bf16[8,128,128]{2,1,0:T(8,128)(2,1)S(1)}, u32[]{:S(2)}, u32[]{:S(2)}) collective-permute-start(bf16[8,128,128]{2,1,0:T(8,128)(2,1)S(1)} %get-tuple-element.30), channel_id=1, source_target_pairs={{4,0},{5,1},{6,2},{7,3},{12,8},{13,9},{14,10},{15,11},{20,16},{21,... | collective-permute-start | bytes 786440 | tf_op jit(solution)/shard_map/ppermute | solution.py:244
  22.3 3.2 %near.1 = (bf16[2,4,1024,128]{3,2,1,0:T(8,128)(2,1)S(1)}, f32[8,128,128]{2,1,0:T(8,128)S(1)}, bf16[128,32,128]{2,1,0:T(8,128)(2,1)S(1)}) custom-call(s32[8,128]{1,0:T(8,128)S(1)} %bitcast.4, bf16[2,2,4,1024,128]{4,3,2,1,0:T(8,128)(2,1)S(1)} %get-tuple-element.19.refs_1_, ...), custom_call_target="tpu_custom_call", output_to_operand_aliasing={{0}: (4, {})} | custom-call | flops 10000000000 | bytes 10000000 | tf_op jit(solution)/shard_map/near/pallas_call | solution.py:37
  25.5 0.1 collective-permute-start.6
  25.6 1.0 %query_own.1.refs_0_ = f32[128,32,128]{2,1,0:T(8,128)S(1)} custom-call(bf16[2,4,1024,128]{3,2,1,0:T(8,128)(2,1)S(1)} %get-tuple-element.26.refs_0_, bf16[2,4,1024,128]{3,2,1,0:T(8,128)(2,1)S(1)} %get-tuple-element.23.refs_4_.refs_6_.refs_1_, bf16[2,4,1024,128]{3,2,1,0:T(8,128)(2,1)S(1)} %get-tuple-element.25.refs_7_.refs_2_, ...), custom_call_target="tpu_custom_call" | custom-call | flops 10000000000 | bytes 10000000 | tf_op jit(solution)/shard_map/query_own/pallas_call | solution.py:37
  26.6 2.1 %collective-permute-done.7 = bf16[8,128,128]{2,1,0:T(8,128)(2,1)S(1)} collective-permute-done((bf16[8,128,128]{2,1,0:T(8,128)(2,1)S(1)}, bf16[8,128,128]{2,1,0:T(8,128)(2,1)S(1)}, u32[]{:S(2)}, u32[]{:S(2)}) %collective-permute-start.7) | collective-permute-done | bytes 262176 | tf_op jit(solution)/shard_map/ppermute | solution.py:244
  28.7 11.8 %collective-permute-done.8 = bf16[8,128,128]{2,1,0:T(8,128)(2,1)S(1)} collective-permute-done((bf16[8,128,128]{2,1,0:T(8,128)(2,1)S(1)}, bf16[8,128,128]{2,1,0:T(8,128)(2,1)S(1)}, u32[]{:S(2)}, u32[]{:S(2)}) %collective-permute-start.8) | collective-permute-done | bytes 262176 | tf_op jit(solution)/shard_map/ppermute | solution.py:244
  40.5 0.1 convert_add_fusion.refs_2_
  40.6 0.0 collective-permute-done.6.refs_1_
  40.6 1.5 %sums.1 = (bf16[128,32,128]{2,1,0:T(8,128)(2,1)}, bf16[128,4,128]{2,1,0:T(4,128)(2,1)}, bf16[128,4,128]{2,1,0:T(4,128)(2,1)}) custom-call(f32[128,32,128]{2,1,0:T(8,128)S(1)} %query_own.1.refs_0_, bf16[128,32,128]{2,1,0:T(8,128)(2,1)S(1)} %collective-permute-done.6.refs_1_, f32[8,128,128]{2,1,0:T(8,128)S(1)} %convert_add_fusion.refs_2_), custom_call_target="tpu_custom_call" | custom-call | flops 10000000000 | bytes 10000000 | tf_op jit(solution)/shard_map/sums/pallas_call | solution.py:37
Async XLA Ops:
  0.6 7.6 %collective-permute-start = (bf16[128,32,128]{2,1,0:T(8,128)(2,1)}, bf16[128,32,128]{2,1,0:T(8,128)(2,1)S(1)}, u32[]{:S(2)}, u32[]{:S(2)}) collective-permute-start(bf16[128,32,128]{2,1,0:T(8,128)(2,1)} %refs_0_.4), channel_id=1, source_target_pairs={{0,1},{1,0},{2,3},{3,2},{4,5},{5,4},{6,7},{7,6},{8,9},{9,8},{10,11... | collective-permute-start | bytes 3145736 | tf_op jit(solution)/shard_map/ppermute | solution.py:240
  1.1 7.1 %collective-permute-start.1 = (bf16[128,32,128]{2,1,0:T(8,128)(2,1)}, bf16[128,32,128]{2,1,0:T(8,128)(2,1)S(1)}, u32[]{:S(2)}, u32[]{:S(2)}) collective-permute-start(bf16[128,32,128]{2,1,0:T(8,128)(2,1)} %refs_1_.4), channel_id=1, source_target_pairs={{0,1},{1,0},{2,3},{3,2},{4,5},{5,4},{6,7},{7,6},{8,9},{9,8},{10,11... | collective-permute-start | bytes 3145736 | tf_op jit(solution)/shard_map/ppermute | solution.py:240
  1.2 7.0 %collective-permute-start.2 = (bf16[128,32,128]{2,1,0:T(8,128)(2,1)}, bf16[128,32,128]{2,1,0:T(8,128)(2,1)S(1)}, u32[]{:S(2)}, u32[]{:S(2)}) collective-permute-start(bf16[128,32,128]{2,1,0:T(8,128)(2,1)} %refs_2_.3), channel_id=1, source_target_pairs={{0,1},{1,0},{2,3},{3,2},{4,5},{5,4},{6,7},{7,6},{8,9},{9,8},{10,11... | collective-permute-start | bytes 3145736 | tf_op jit(solution)/shard_map/ppermute | solution.py:240
  1.7 6.6 %collective-permute-start.3 = (f32[32,128]{1,0:T(8,128)}, f32[32,128]{1,0:T(8,128)S(1)}, u32[]{:S(2)}, u32[]{:S(2)}) collective-permute-start(f32[32,128]{1,0:T(8,128)} %refs_3_.3), channel_id=1, source_target_pairs={{0,1},{1,0},{2,3},{3,2},{4,5},{5,4},{6,7},{7,6},{8,9},{9,8},{10,11... | collective-permute-start | bytes 49160 | tf_op jit(solution)/shard_map/ppermute | solution.py:240
  3.3 7.8 %copy-start = (s32[1024]{0:T(1024)S(1)}, s32[1024]{0:T(1024)}, u32[]{:S(2)}) copy-start(s32[1024]{0:T(1024)} %param.13) | copy-start | bytes 12292
  3.3 11.0 %collective-permute-start.4 = (bf16[8,128,128]{2,1,0:T(8,128)(2,1)S(1)}, bf16[8,128,128]{2,1,0:T(8,128)(2,1)S(1)}, u32[]{:S(2)}, u32[]{:S(2)}) collective-permute-start(bf16[8,128,128]{2,1,0:T(8,128)(2,1)S(1)} %pack.1.refs_3_), channel_id=1, source_target_pairs={{0,2},{1,3},{2,4},{3,5},{4,6},{5,7},{8,10},{9,11},{10,12},{11,13},... | collective-permute-start | bytes 786440 | tf_op jit(solution)/shard_map/ppermute | solution.py:244
  12.8 7.1 %collective-permute-start.5 = (bf16[8,128,128]{2,1,0:T(8,128)(2,1)S(1)}, bf16[8,128,128]{2,1,0:T(8,128)(2,1)S(1)}, u32[]{:S(2)}, u32[]{:S(2)}) collective-permute-start(bf16[8,128,128]{2,1,0:T(8,128)(2,1)S(1)} %get-tuple-element.24), channel_id=1, source_target_pairs={{0,4},{1,5},{2,6},{3,7},{8,12},{9,13},{10,14},{11,15},{16,20},{17,... | collective-permute-start | bytes 786440 | tf_op jit(solution)/shard_map/ppermute | solution.py:244
  15.2 13.5 %collective-permute-start.7 = (bf16[8,128,128]{2,1,0:T(8,128)(2,1)S(1)}, bf16[8,128,128]{2,1,0:T(8,128)(2,1)S(1)}, u32[]{:S(2)}, u32[]{:S(2)}) collective-permute-start(bf16[8,128,128]{2,1,0:T(8,128)(2,1)S(1)} %get-tuple-element.29), channel_id=1, source_target_pairs={{2,0},{3,1},{4,2},{5,3},{6,4},{7,5},{10,8},{11,9},{12,10},{13,11},... | collective-permute-start | bytes 786440 | tf_op jit(solution)/shard_map/ppermute | solution.py:244
  21.0 19.4 %collective-permute-start.8 = (bf16[8,128,128]{2,1,0:T(8,128)(2,1)S(1)}, bf16[8,128,128]{2,1,0:T(8,128)(2,1)S(1)}, u32[]{:S(2)}, u32[]{:S(2)}) collective-permute-start(bf16[8,128,128]{2,1,0:T(8,128)(2,1)S(1)} %get-tuple-element.30), channel_id=1, source_target_pairs={{4,0},{5,1},{6,2},{7,3},{12,8},{13,9},{14,10},{15,11},{20,16},{21,... | collective-permute-start | bytes 786440 | tf_op jit(solution)/shard_map/ppermute | solution.py:244
  25.5 15.1 %collective-permute-start.6 = (bf16[128,32,128]{2,1,0:T(8,128)(2,1)S(1)}, bf16[128,32,128]{2,1,0:T(8,128)(2,1)S(1)}, u32[]{:S(2)}, u32[]{:S(2)}) collective-permute-start(bf16[128,32,128]{2,1,0:T(8,128)(2,1)S(1)} %get-tuple-element.27), channel_id=1, source_target_pairs={{0,1},{1,0},{2,3},{3,2},{4,5},{5,4},{6,7},{7,6},{8,9},{9,8},{10,11... | collective-permute-start | bytes 3145736 | tf_op jit(solution)/shard_map/ppermute | solution.py:240
